TPU v7x, 32 devices: a whole 2x2x4 slice. The times are simulated.
32 devices in a mesh: seq: 16 (over z, y, x), tp: 2 (over core).
Axes of the slice: x: 2, y: 2, z: 4, core: 2. Of those that a mesh axis runs over, the one named last changes fastest.
Arguments:
- layer_input: bfloat16 [4096, 2048], P('seq'), may hold values from -1.5 to 1.5
- query: bfloat16 [4096, 2048], P('seq', 'tp'), may hold values from -6 to 6
- suffix_kv: bfloat16 [2, 4096, 2048], P(None, 'seq', 'tp'), may hold values from -6 to 6
- prefix_kv: bfloat16 [2, 512, 2048], P(None, 'seq', 'tp'), may hold values from -6 to 6
- node_len: int32 [16], replicated, may hold values from 8 to 32, as said below
- path: int32 [16, 3], P('seq'), may hold values from 0 to 15, as said below
- out_weight: bfloat16 [2048, 2048], P('tp'), may hold values from -0.125 to 0.125
- norm_gain: float32 [2048], replicated, may hold values from 0.1 to 1.9
- expert_ids: int32 [4096, 8], P('seq'), may hold values from 0 to 15, all different within a row; in each aligned block of 256 rows (0 to 255, 256 to 511, ...) at most 160 rows name the same one
- gates: float32 [4096, 8], P('seq'), may hold values from 0.1 to 0.4
- w_gate: bfloat16 [16, 2048, 1024], P('seq', None, 'tp'), may hold values from -0.125 to 0.125
- w_up: bfloat16 [16, 2048, 1024], P('seq', None, 'tp'), may hold values from -0.125 to 0.125
- w_down: bfloat16 [16, 1024, 2048], P('seq', 'tp'), may hold values from -0.1875 to 0.1875
Outputs:
- layer_out: bfloat16 [4096, 2048], P('seq', 'tp')
Inputs may be any that keep to these rules, and one draw needn't show every extreme that they name: `path`: row r names three different nodes. Nodes are of three levels: roots, middle nodes and leaves; a middle node always comes with the same root, a leaf always with the same middle node, and every node is named by some request. `node_len`: some node holds exactly 32 tokens. `expert_ids`: within the 256 rows of one request no expert is named more than 160 times, a bound that some block reaches.
All inputs are finite; a program needn't handle non-finite values.
Results may differ from a plain program's by a relative error of at most 0.019.
Values may be sent and summed in bfloat16 or wider, within the bound.
A program may use at most 128 MiB of HBM per device.

v0:
```python
import math

import jax
import jax.numpy as jnp
from jax import lax
from jax.sharding import PartitionSpec as P

D = 2048
HD = 128
TOPK = 8
SLOT = 32


def slot_plan(ids, experts, cap):
    flat = ids.reshape(-1)
    onehot = (flat[:, None] == jnp.arange(experts, dtype=jnp.int32)[None, :]).astype(jnp.int32)
    rank = jnp.sum(jnp.cumsum(onehot, axis=0) * onehot, axis=1) - 1
    return flat * cap + rank


def local(
    layer_input,
    query,
    suffix_kv,
    prefix_kv,
    node_len,
    path,
    out_weight,
    norm_gain,
    expert_ids,
    gates,
    w_gate,
    w_up,
    w_down,
):
    rows = query.shape[0]
    heads_here = query.shape[1] // HD
    scale = 1.0 / math.sqrt(HD)
    queries = query.reshape(rows, heads_here, HD)
    own_keys = suffix_kv[0].reshape(rows, heads_here, HD)
    own_values = suffix_kv[1].reshape(rows, heads_here, HD).astype(jnp.float32)
    scores = (
        jnp.einsum("qhd,khd->hqk", queries, own_keys, preferred_element_type=jnp.float32) * scale
    )
    top = jnp.max(scores, axis=2)
    probs = jnp.exp(scores - top[:, :, None])
    total = jnp.sum(probs, axis=2)
    accum = jnp.einsum("hqk,khd->hqd", probs, own_values)
    my_nodes = path[0]
    node_ids = jnp.arange(node_len.shape[0], dtype=jnp.int32)
    piece = lax.all_gather(prefix_kv, "seq", axis=1, tiled=True)
    start = jnp.int32(0)
    count = piece.shape[1]

    def absorb(state):
        best, mass, sums = state
        index = jnp.arange(count, dtype=jnp.int32)
        node = index // SLOT
        offset = index % SLOT
        match = node[:, None] == node_ids[None, :]
        lengths = jnp.sum(jnp.where(match, node_len[None, :], 0), axis=1)
        live = (offset < lengths) & jnp.any(node[:, None] == my_nodes[None, :], axis=1)
        piece_keys = piece[0].reshape(count, heads_here, HD)
        piece_values = piece[1].reshape(count, heads_here, HD).astype(jnp.float32)
        block = (
            jnp.einsum("qhd,khd->hqk", queries, piece_keys, preferred_element_type=jnp.float32)
            * scale
        )
        block = jnp.where(live[None, None, :], block, -jnp.inf)
        new_best = jnp.maximum(best, jnp.max(block, axis=2))
        weights = jnp.exp(block - new_best[:, :, None])
        factor = jnp.exp(best - new_best)
        new_mass = mass * factor + jnp.sum(weights, axis=2)
        new_sums = sums * factor[:, :, None] + jnp.einsum("hqk,khd->hqd", weights, piece_values)
        return (new_best, new_mass, new_sums)

    node_start = my_nodes * SLOT
    touched = jnp.any((node_start + SLOT > start) & (node_start < start + count))
    top, total, accum = lax.cond(touched, absorb, lambda state: state, (top, total, accum))
    attn = (accum / total[:, :, None]).astype(jnp.bfloat16)
    partial_value = jnp.einsum(
        "hqd,hdm->qm",
        attn,
        out_weight.reshape(heads_here, HD, D),
        preferred_element_type=jnp.float32,
    )
    tp_index = lax.axis_index("tp")
    tp_count = lax.axis_size("tp")
    half = D // tp_count
    experts = w_gate.shape[0] * lax.axis_size("seq")
    cap = 5 * rows * TOPK // (4 * experts)
    dest = slot_plan(expert_ids, experts, cap)
    hidden_state = layer_input.astype(jnp.float32) + lax.psum(partial_value, "tp")
    mean_square = jnp.mean(hidden_state * hidden_state, axis=1, keepdims=True)
    normed = (hidden_state * lax.rsqrt(mean_square + 1e-06) * norm_gain).astype(jnp.bfloat16)
    spread = jnp.repeat(normed, TOPK, axis=0)
    outgoing = (
        jnp.zeros((experts * cap, D), jnp.bfloat16).at[dest].set(spread).reshape(experts, cap, D)
    )
    arrived = lax.all_to_all(outgoing, "seq", split_axis=0, concat_axis=0, tiled=True)
    sources = arrived.shape[0]
    items = arrived.shape[1]
    flat = arrived.reshape(sources * items, D)
    gate_part = jnp.dot(flat, w_gate[0], preferred_element_type=jnp.float32)
    up_part = jnp.dot(flat, w_up[0], preferred_element_type=jnp.float32)
    act = (jax.nn.silu(gate_part) * up_part).astype(jnp.bfloat16)
    terms = jnp.dot(act, w_down[0], preferred_element_type=jnp.float32).reshape(sources, items, D)
    summed = lax.psum_scatter(terms, "tp", scatter_dimension=2, tiled=True).astype(jnp.bfloat16)
    back = lax.all_to_all(summed, "seq", split_axis=0, concat_axis=0, tiled=True)
    residual = lax.dynamic_slice_in_dim(hidden_state, tp_index * half, half, 1)
    results = back.reshape(experts * cap, half)[dest].reshape(rows, TOPK, half).astype(jnp.float32)
    mixture = jnp.sum(gates[:, :, None] * results, axis=1)
    return (residual + mixture).astype(jnp.bfloat16)


def solution(mesh):
    in_specs = (
        P("seq", None),
        P("seq", "tp"),
        P(None, "seq", "tp"),
        P(None, "seq", "tp"),
        P(),
        P("seq", None),
        P("tp", None),
        P(),
        P("seq", None),
        P("seq", None),
        P("seq", None, "tp"),
        P("seq", None, "tp"),
        P("seq", "tp", None),
    )
    out_specs = P("seq", "tp")
    return jax.shard_map(local, mesh=mesh, in_specs=in_specs, out_specs=out_specs, check_vma=False)
```

profile of v0, /device:TPU:14, one launch (start us, length us, event | category | flops | bytes accessed | tf_op | source)
XLA Modules:
  0.0 579.5 jit_solution(16960547954099875234)
XLA Ops:
  6.5 1.8 copy.57
  8.5 2.1 fusion.37
  10.5 1.0 copy.71
  11.5 1.2 copy.50
  12.8 1.2 copy.72
  14.0 0.6 and_reduce_fusion
  15.3 1.5 multiply_reduce_fusion.1
  16.9 0.4 fusion.28
  17.2 1.6 fusion.27
  18.8 52.3 %all-gather.2.cloned.1.call-done = bf16[2,512,1024]{2,0,1:T(2,128)(2,1)} async-done(((bf16[2,32,1024]{2,0,1:T(2,128)(2,1)}), bf16[2,512,1024]{2,0,1:T(2,128)(2,1)}) %all-gather.2.cloned.1.call-update) | async-done | bytes 2097168 | tf_op jit(solution)/shard_map/all_gather | solution.py:51
  71.1 12.6 %conditional.1 = ((f32[8,256]{1,0:T(8,128)S(1)}, f32[8,256,128]{2,1,0:T(8,128)})) conditional(s32[]{:T(128)} %convert_element_type.35, (f32[8,256]{1,0:T(8,128)S(1)}, f32[8,256,128]{2,1,0:T(8,128)}) %tuple.12, (s32[16]{0:T(128)S(1)}, s32[16]{0:T(128)S(1)}, s32[1,3]{1,0:T(1,128)S(1)}, bf16[2,512,1024]{2,0,1:T(2,128)(2,1)}, ...), branch_computations={%region_3.0_spmd, %region_4.9_spmd} | conditional | flops 547919872 | bytes 34206940 | solution.py:79
  71.1 0.1 select_reduce_fusion
  71.2 0.1 compare_reduce_fusion
  71.3 6.1 %copy.58 = bf16[2,512,1024]{1,2,0:T(8,128)(2,1)} copy(bf16[2,512,1024]{2,0,1:T(2,128)(2,1)} %get-tuple-element.58) | data formatting | bytes 4194304 | tf_op jit(solution)/shard_map
  77.4 1.7 fusion.36
  79.1 0.8 fusion
  80.0 1.2 fusion.2
  81.3 1.5 fusion.7
  82.7 1.0 copy-done.4
  83.7 5.3 convolution_bitcast_fusion
  89.0 0.2 reduce-scatter.2.cloned.1.call-start
  89.2 0.1 copy.62
  89.4 0.1 eq.59
  89.5 0.1 eq.55
  89.6 4.5 reduce-window.6
  94.2 0.4 slice_reduce_fusion
  94.6 0.2 reduce-window.9
  94.8 0.1 copy.61
  94.9 0.1 mul.87
  95.0 0.1 broadcast_add_fusion
  95.1 0.1 fusion.33
  95.2 15.0 %all-reduce.2.cloned.1.call-done = f32[256,2048]{1,0:T(8,128)} async-done(((f32[256,2048]{1,0:T(8,128)}), f32[256,2048]{1,0:T(8,128)}) %all-reduce.2.cloned.1.call-update) | async-done | bytes 2097168 | tf_op jit(solution)/shard_map/psum | solution.py:93
  110.2 1.9 multiply_reduce_fusion
  112.2 1.3 copy-done.1
  113.5 0.2 multiply_convert_fusion.1
  113.7 18.1 %scatter_custom_fusion = bf16[2560,2048]{1,0:T(8,128)(2,1)} fusion(s32[2048]{0:T(1024)S(1)} %bitcast.65, bf16[]{:T(256)} %constant.78.clone.1, bf16[256,2048]{1,0:T(8,128)(2,1)S(1)} %multiply_convert_fusion.1), kind=kCustom, calls=%fused_computation.32 | custom fusion | bytes 11534338 | tf_op jit(solution)/shard_map/scatter | solution.py:98
  131.8 234.0 %all_to_all.10 = bf16[16,160,2048]{2,1,0:T(8,128)(2,1)S(1)} all-to-all(bf16[16,160,2048]{2,1,0:T(8,128)(2,1)} %bitcast.55), channel_id=1, replica_groups=mesh['seq'=16,'tp'=2] {'seq'}, dimensions={0} | all-to-all | bytes 20971520 | tf_op jit(solution)/shard_map/all_to_all | solution.py:100
  365.8 5.7 fusion.25
  371.5 6.7 %multiply_convert_fusion = bf16[2560,512]{1,0:T(8,128)(2,1)S(1)} fusion(f32[2560,512]{1,0:T(8,128)S(1)} %fusion.25, bf16[2560,2048]{1,0:T(8,128)(2,1)S(1)} %bitcast.57, bf16[1,2048,512]{2,1,0:T(8,128)(2,1)S(1)} %copy-done.12), kind=kOutput, calls=%fused_computation.34 | convolution fusion | flops 5376573440 | bytes 20447232 | tf_op jit(solution)/shard_map/dot_general | solution.py:105
  378.2 10.0 %fusion.22 = f32[16,160,2048]{2,1,0:T(8,128)} fusion(bf16[16,160,512]{2,1,0:T(8,128)(2,1)S(1)} %bitcast.71, bf16[1,512,2048]{2,1,0:T(8,128)(2,1)S(1)} %copy-done), kind=kOutput, calls=%fused_computation.38 | convolution fusion | flops 5368709120 | bytes 25690112 | tf_op jit(solution)/shard_map/dot_general | solution.py:107
  388.2 31.1 %reduce-scatter.2.cloned.1.call-done = f32[16,160,1024]{2,1,0:T(8,128)} async-done(((f32[16,160,2048]{2,1,0:T(8,128)}), f32[16,160,1024]{2,1,0:T(8,128)}) %reduce-scatter.2.cloned.1.call-update) | async-done | bytes 10485776 | tf_op jit(solution)/shard_map/reduce_scatter | solution.py:108
  419.3 7.2 %convert_element_type.40 = bf16[16,160,1024]{2,1,0:T(8,128)(2,1)} convert(f32[16,160,1024]{2,1,0:T(8,128)} %reduce-scatter.2.cloned.1.call-done) | non-fusion elementwise | flops 2621440 | bytes 15728640 | tf_op jit(solution)/shard_map/convert_element_type | solution.py:108
  426.5 7.1 %all-to-all-start.1 = ((bf16[16,160,1024]{2,1,0:T(8,128)(2,1)}), bf16[16,160,1024]{2,1,0:T(8,128)(2,1)}, u32[]{:S(2)}, u32[]{:S(2)}) async-start(bf16[16,160,1024]{2,1,0:T(8,128)(2,1)} %convert_element_type.40), calls=%async_computation.2 | async-start | bytes 10485760 | tf_op jit(solution)/shard_map/all_to_all | solution.py:109
  433.6 0.1 copy.60
  433.7 119.1 %all-to-all-done.1 = bf16[16,160,1024]{2,1,0:T(8,128)(2,1)} async-done(((bf16[16,160,1024]{2,1,0:T(8,128)(2,1)}), bf16[16,160,1024]{2,1,0:T(8,128)(2,1)}, u32[]{:S(2)}, u32[]{:S(2)}) %all-to-all-start.1) | async-done | bytes 5242912 | tf_op jit(solution)/shard_map/all_to_all | solution.py:109
  552.9 14.2 %gather_fusion = bf16[2048,1024]{1,0:T(8,128)(2,1)} fusion(bf16[2560,1024]{1,0:T(8,128)(2,1)} %bitcast.19, s32[2048]{0:T(1024)S(1)} %broadcast_clamp_fusion), kind=kCustom, calls=%fused_computation | custom fusion | bytes 8396800 | tf_op jit(solution)/shard_map/gather | solution.py:111
  567.1 4.9 fusion.17
  572.0 0.9 add_convert_fusion
  (40 shorter events, 0.2 us)
Async XLA Ops:
  6.5 371.7 %copy-start = (bf16[1,512,2048]{2,1,0:T(8,128)(2,1)S(1)}, bf16[1,512,2048]{2,1,0:T(8,128)(2,1)}, u32[]{:S(2)}) copy-start(bf16[1,512,2048]{2,1,0:T(8,128)(2,1)} %param.27) | copy-start | bytes 6291460
  6.5 7.5 %copy-start.10 = (s32[1,3]{1,0:T(1,128)S(1)}, s32[1,3]{1,0:T(1,128)}, u32[]{:S(2)}) copy-start(s32[1,3]{1,0:T(1,128)} %param.20) | copy-start | bytes 40
  6.5 64.6 %all-gather.2.cloned.1.call-start = ((), (), s32[]{:S(2)}) async-start(), calls=%async_computation.3 | async-start | bytes 2228224 | tf_op jit(solution)/shard_map/all_gather | solution.py:51
  8.4 101.8 %all-reduce.2.cloned.1.call-start = ((), (), s32[]{:S(2)}) async-start(), calls=%async_computation.4 | async-start | bytes 4194304 | tf_op jit(solution)/shard_map/psum | solution.py:93
  15.3 55.8 %copy-start.9 = (s32[16]{0:T(128)S(1)}, s32[16]{0:T(128)}, u32[]{:S(2)}) copy-start(s32[16]{0:T(128)} %param.19) | copy-start | bytes 196
  79.1 2.1 copy-start.3
  82.7 1.0 copy-start.4
  83.7 5.5 copy-start.6
  83.7 26.5 %copy-start.5 = (bf16[256,2048]{1,0:T(8,128)(2,1)S(1)}, bf16[256,2048]{1,0:T(8,128)(2,1)}, u32[]{:S(2)}) copy-start(bf16[256,2048]{1,0:T(8,128)(2,1)} %param.15) | copy-start | bytes 3145732
  89.0 24.5 %copy-start.7 = (f32[2048]{0:T(1024)S(1)}, f32[2048]{0:T(1024)}, u32[]{:S(2)}) copy-start(f32[2048]{0:T(1024)} %param.22) | copy-start | bytes 24580
  89.0 330.3 %reduce-scatter.2.cloned.1.call-start = ((), (), s32[]{:S(2)}) async-start(), calls=%async_computation.5 | async-start | bytes 31457280 | tf_op jit(solution)/shard_map/reduce_scatter | solution.py:108
  112.2 1.3 copy-start.1
  131.8 234.0 %copy-start.11 = (bf16[1,2048,512]{2,1,0:T(8,128)(2,1)S(1)}, bf16[1,2048,512]{2,1,0:T(8,128)(2,1)}, u32[]{:S(2)}) copy-start(bf16[1,2048,512]{2,1,0:T(8,128)(2,1)} %param.25) | copy-start | bytes 6291460
  365.8 5.7 copy-start.12
  426.5 7.1 %copy-start.8 = (f32[256,8]{0,1:T(8,128)S(1)}, f32[256,8]{0,1:T(8,128)}, u32[]{:S(2)}) copy-start(f32[256,8]{0,1:T(8,128)} %param.24) | copy-start | bytes 24580
  426.5 126.4 %all-to-all-start.1 = ((bf16[16,160,1024]{2,1,0:T(8,128)(2,1)}), bf16[16,160,1024]{2,1,0:T(8,128)(2,1)}, u32[]{:S(2)}, u32[]{:S(2)}) async-start(bf16[16,160,1024]{2,1,0:T(8,128)(2,1)} %convert_element_type.40), calls=%async_computation.2 | async-start | bytes 10485760 | tf_op jit(solution)/shard_map/all_to_all | solution.py:109
  567.0 4.9 copy-start.2
Sparse Core Ops, SparseCore 0:
  10.1 60.9 all-gather.1
  89.1 21.0 all-reduce.1
  388.3 30.9 reduce-scatter.1
where the time goes:
time: 580 us; the launch traced here: 579 us
  blocking collectives  234 us (40%)
  waiting for transfers between devices  218 us (38%)
  local copies, waits for them, and re-layouts  50.9 us (9%)
  matrix products  33 us (6%)
  other arithmetic  22.6 us (4%)
  between operations  14 us (2%)
  starting transfers between devices  7.36 us (1%)
    all_to_all x1, blocking collectives, local(): lax.all_to_all(outgoing, 'seq', split_axis=0, concat_axis=0, tiled=True)  234 us
    all_to_all x1, waiting for transfers between devices, local(): lax.all_to_all(summed, 'seq', split_axis=0, concat_axis=0, tiled=True)  119 us
    all_gather x1, waiting for transfers between devices, local(): piece = lax.all_gather(prefix_kv, 'seq', axis=1, tiled=True)  52.3 us
    reduce_scatter x1, waiting for transfers between devices, local(): lax.psum_scatter(terms, 'tp', scatter_dimension=2, tiled=True)  31.1 us
    scatter x1, local copies, waits for them, and re-layouts, local(): jnp.zeros((experts * cap, D), jnp.bfloat16).at[dest].set(spread)  18.1 us
    psum x1, waiting for transfers between devices, local(): lax.psum(partial_value, 'tp')  15 us
    gather x1, local copies, waits for them, and re-layouts, local(): back.reshape(experts * cap, half)[dest].reshape(rows, TOPK, half)  14.2 us
  transfers between devices with their start and end apart: 4, of which 4 were waited for; matrix products, arithmetic and copies ran while one was open for 3% of the time, Pallas kernels for 0%

commit v1 on v0

--- a/solution.py
+++ b/solution.py
@@ -9,6 +9,7 @@
 HD = 128
 TOPK = 8
 SLOT = 32
+DENSE_SEQ = 16
 
 
 def slot_plan(ids, experts, cap):
@@ -16,6 +17,24 @@
     onehot = (flat[:, None] == jnp.arange(experts, dtype=jnp.int32)[None, :]).astype(jnp.int32)
     rank = jnp.sum(jnp.cumsum(onehot, axis=0) * onehot, axis=1) - 1
     return flat * cap + rank
+
+
+def dense_experts(normed, expert_ids, gates, w_gate, w_up, w_down, tp_index, half):
+    mine = lax.axis_index("seq")
+    experts = lax.axis_size("seq")
+    named = expert_ids[:, :, None] == jnp.arange(experts, dtype=jnp.int32)[None, None, :]
+    table = jnp.sum(jnp.where(named, gates[:, :, None], 0.0), axis=1)
+    table = lax.all_gather(table, "seq", axis=0, tiled=True)
+    weight = lax.dynamic_slice_in_dim(table, mine, 1, 1)
+    part = lax.dynamic_slice_in_dim(normed, tp_index * half, half, 1)
+    column = lax.all_gather(part, "seq", axis=0, tiled=True)
+    tokens = lax.all_gather(column, "tp", axis=1, tiled=True)
+    gate_part = jnp.dot(tokens, w_gate[0], preferred_element_type=jnp.float32)
+    up_part = jnp.dot(tokens, w_up[0], preferred_element_type=jnp.float32)
+    act = (jax.nn.silu(gate_part) * up_part).astype(jnp.bfloat16)
+    terms = jnp.dot(act, w_down[0], preferred_element_type=jnp.float32) * weight
+    terms = lax.psum_scatter(terms.astype(jnp.bfloat16), "tp", scatter_dimension=1, tiled=True)
+    return lax.psum_scatter(terms, "seq", scatter_dimension=0, tiled=True).astype(jnp.float32)
 
 
 def local(
@@ -93,6 +112,10 @@
     hidden_state = layer_input.astype(jnp.float32) + lax.psum(partial_value, "tp")
     mean_square = jnp.mean(hidden_state * hidden_state, axis=1, keepdims=True)
     normed = (hidden_state * lax.rsqrt(mean_square + 1e-06) * norm_gain).astype(jnp.bfloat16)
+    if lax.axis_size("seq") <= DENSE_SEQ:
+        mixture = dense_experts(normed, expert_ids, gates, w_gate, w_up, w_down, tp_index, half)
+        residual = lax.dynamic_slice_in_dim(hidden_state, tp_index * half, half, 1)
+        return (residual + mixture).astype(jnp.bfloat16)
     spread = jnp.repeat(normed, TOPK, axis=0)
     outgoing = (
         jnp.zeros((experts * cap, D), jnp.bfloat16).at[dest].set(spread).reshape(experts, cap, D)

time: 580 us -> 525 us (0.905)
  blocking collectives: 234 us -> 30.7 us
  waiting for transfers between devices: 218 us -> 399 us
  local copies, waits for them, and re-layouts: 50.9 us -> 19.4 us
  matrix products: 33 us -> 51 us
  other arithmetic: 22.6 us -> 8.37 us
  starting transfers between devices: 7.36 us -> 0.21 us
    all_to_all x1 -> x0, blocking collectives: 234 us -> none  [local(): lax.all_to_all(outgoing, 'seq', split_axis=0, concat_axis=0, tiled=True)]
    reduce_scatter x1 -> x2, waiting for transfers between devices: 31.1 us -> 215 us  [the longest x1 182 us: dense_experts(): lax.psum_scatter(terms, 'seq', scatter_dimension=0, tiled=True)]
    all_to_all x1 -> x0, waiting for transfers between devices: 119 us -> none  [local(): lax.all_to_all(summed, 'seq', split_axis=0, concat_axis=0, tiled=True)]
    all_gather x0 -> x2, waiting for transfers between devices: none -> 112 us  [the longest x1 112 us: dense_experts(): column = lax.all_gather(part, 'seq', axis=0, tiled=True)]
    all_gather x0 -> x1, blocking collectives: none -> 30.7 us  [dense_experts(): table = lax.all_gather(table, 'seq', axis=0, tiled=True)]
    scatter x1 -> x0, local copies, waits for them, and re-layouts: 18.1 us -> none  [local(): jnp.zeros((experts * cap, D), jnp.bfloat16).at[dest].set(spread)]
    dot_general x3 -> x2, matrix products: 22.3 us -> 40.3 us  [the longest x1 25.3 us: dense_experts(): terms = jnp.dot(act, w_down[0], preferred_element_type=jnp.float32) * weight]
    gather x1 -> x0, local copies, waits for them, and re-layouts: 14.2 us -> none  [local(): back.reshape(experts * cap, half)[dest].reshape(rows, TOPK, half)]
  transfers between devices with their start and end apart: 4 -> 6, of which waited for: 4 -> 6; matrix products, arithmetic and copies ran while one was open for 3% -> 2% of each run, Pallas kernels for 0% -> 0%
where the time goes in v1:
time: 525 us; the launch traced here: 523 us
  waiting for transfers between devices  399 us (76%)
  matrix products  51 us (10%)
  blocking collectives  30.7 us (6%)
  local copies, waits for them, and re-layouts  19.4 us (4%)
  between operations  14.2 us (3%)
  other arithmetic  8.37 us (2%)
    reduce_scatter x1, waiting for transfers between devices, dense_experts(): lax.psum_scatter(terms, 'seq', scatter_dimension=0, tiled=True)  182 us
    all_gather x1, waiting for transfers between devices, dense_experts(): column = lax.all_gather(part, 'seq', axis=0, tiled=True)  112 us
    all_gather x1, waiting for transfers between devices, local(): piece = lax.all_gather(prefix_kv, 'seq', axis=1, tiled=True)  50.4 us
    reduce_scatter x1, waiting for transfers between devices, dense_experts(): lax.psum_scatter(terms.astype(jnp.bfloat16), 'tp', scatter_dimension=1, t...  32.7 us
    all_gather x1, blocking collectives, dense_experts(): table = lax.all_gather(table, 'seq', axis=0, tiled=True)  30.7 us
    dot_general x1, matrix products, dense_experts(): terms = jnp.dot(act, w_down[0], preferred_element_type=jnp.float32) * weight  25.3 us
    psum x1, waiting for transfers between devices, local(): lax.psum(partial_value, 'tp')  21.1 us
    dot_general x1, matrix products, dense_experts(): gate_part = jnp.dot(tokens, w_gate[0], preferred_element_type=jnp.float32)  15 us
  transfers between devices with their start and end apart: 6, of which 6 were waited for; matrix products, arithmetic and copies ran while one was open for 2% of the time, Pallas kernels for 0%

profile of v1, /device:TPU:14, one launch (start us, length us, event | category | flops | bytes accessed | tf_op | source)
XLA Modules:
  0.0 522.8 jit_solution(10051002971987933823)
XLA Ops:
  6.5 1.8 copy.54
  8.4 0.0 all-gather.4.cloned.1.call-update
  8.4 0.0 all-reduce.2.cloned.1.call-start
  8.4 1.3 and_reduce_fusion
  10.4 1.2 copy.47
  11.6 2.2 fusion.28
  13.9 1.2 copy.65
  15.1 2.0 copy.64
  17.2 1.6 multiply_reduce_fusion.1
  18.7 0.4 fusion.22
  19.1 1.6 fusion.21
  20.7 50.4 %all-gather.4.cloned.1.call-done = bf16[2,512,1024]{2,0,1:T(2,128)(2,1)} async-done(((bf16[2,32,1024]{2,0,1:T(2,128)(2,1)}), bf16[2,512,1024]{2,0,1:T(2,128)(2,1)}) %all-gather.4.cloned.1.call-update) | async-done | bytes 2097168 | tf_op jit(solution)/shard_map/all_gather | solution.py:70
  71.1 0.0 copy-done.9
  71.1 12.6 %conditional.1 = ((f32[8,256]{1,0:T(8,128)S(1)}, f32[8,256,128]{2,1,0:T(8,128)})) conditional(s32[]{:T(128)} %convert_element_type.27, (f32[8,256]{1,0:T(8,128)S(1)}, f32[8,256,128]{2,1,0:T(8,128)}) %tuple.12, (s32[16]{0:T(128)S(1)}, s32[16]{0:T(128)S(1)}, s32[1,3]{1,0:T(1,128)S(1)}, bf16[2,512,1024]{2,0,1:T(2,128)(2,1)}, ...), branch_computations={%region_3.0_spmd, %region_4.9_spmd} | conditional | flops 547919872 | bytes 34206940 | solution.py:98
  71.1 0.1 compare_reduce_fusion
  71.2 0.1 select_reduce_fusion
  71.3 6.1 %copy.55 = bf16[2,512,1024]{1,2,0:T(8,128)(2,1)} copy(bf16[2,512,1024]{2,0,1:T(2,128)(2,1)} %get-tuple-element.58) | data formatting | bytes 4194304 | tf_op jit(solution)/shard_map
  77.4 1.7 fusion.27
  79.1 0.8 fusion
  80.0 1.2 fusion.2
  81.2 1.5 fusion.7
  82.7 1.0 copy-done.4
  83.7 5.2 %convolution_bitcast_fusion = f32[256,2048]{1,0:T(8,128)} fusion(bf16[8,128,2048]{2,1,0:T(8,128)(2,1)} %bitcast.45, f32[8,256,128]{2,1,0:T(8,128)} %get-tuple-element.35, f32[8,256]{1,0:T(8,128)S(1)} %get-tuple-element.36), kind=kOutput, calls=%fused_computation.30 | convolution fusion | flops 1074266112 | bytes 7348224 | tf_op jit(solution)/shard_map/hqd,hdm->qm/dot_general | solution.py:100
  88.9 0.0 all-reduce.2.cloned.1.call-update
  89.0 0.0 all-gather.6.cloned.1.call-start
  89.0 0.0 dynamic-slice-start
  89.0 21.1 %all-reduce.2.cloned.1.call-done = f32[256,2048]{1,0:T(8,128)} async-done(((f32[256,2048]{1,0:T(8,128)}), f32[256,2048]{1,0:T(8,128)}) %all-reduce.2.cloned.1.call-update) | async-done | bytes 2097168 | tf_op jit(solution)/shard_map/psum | solution.py:112
  110.1 1.9 multiply_reduce_fusion
  112.1 1.3 copy-done.2
  113.4 0.9 multiply_convert_fusion.2
  114.4 0.0 all-gather.6.cloned.1.call-update
  114.4 0.0 all-gather.8.cloned.1.call-start
  114.4 111.8 %all-gather.6.cloned.1.call-done = bf16[4096,1024]{1,0:T(8,128)(2,1)} async-done(((bf16[256,1024]{1,0:T(8,128)(2,1)}), bf16[4096,1024]{1,0:T(8,128)(2,1)}) %all-gather.6.cloned.1.call-update) | async-done | bytes 8388624 | tf_op jit(solution)/shard_map/all_gather | solution.py:30
  226.2 0.0 all-gather.8.cloned.1.call-update
  226.2 0.0 reduce-scatter.3.cloned.1.call-start
  226.3 0.6 copy-done.6
  226.9 0.0 copy-done.7
  226.9 30.7 %all_gather.15 = f32[4096,16]{0,1:T(8,128)S(1)} all-gather(f32[256,16]{0,1:T(8,128)S(1)} %select_reduce_fusion.1), channel_id=1, replica_groups=mesh['seq'=16,'tp'=2] {'seq'}, dimensions={0}, use_global_device_ids=true | all-gather | bytes 278528 | tf_op jit(solution)/shard_map/all_gather | solution.py:27
  257.7 0.7 all-gather.8.cloned.1.call-done
  258.3 15.0 %fusion.19 = f32[4096,512]{1,0:T(8,128)} fusion(bf16[4096,2048]{1,0:T(8,128)(2,1)} %all-gather.8.cloned.1.call-done, bf16[1,2048,512]{2,1,0:T(8,128)(2,1)} %param.25), kind=kOutput, calls=%fused_computation.33 | convolution fusion | flops 8589934592 | bytes 27262976 | tf_op jit(solution)/shard_map/dot_general | solution.py:32
  273.3 0.0 copy-done
  273.3 25.3 %multiply_convert_fusion = bf16[4096,2048]{1,0:T(8,128)(2,1)} fusion(f32[4096]{0:T(1024)S(1)} %bitcast.43, bf16[1,512,2048]{2,1,0:T(8,128)(2,1)S(1)} %copy-done, f32[4096,512]{1,0:T(8,128)} %fusion.19, bf16[4096,2048]{1,0:T(8,128)(2,1)} %all-gather.8.cloned.1.call-done, bf16[1,2048,512]{2,1,0:T(8,128)(2,1)} %param.26), kind=kOutput, calls=%fused_computation.28 | convolution fusion | flops 17209229312 | bytes 46153728 | tf_op jit(solution)/shard_map/dot_general | solution.py:35
  298.6 0.0 reduce-scatter.3.cloned.1.call-update
  298.6 0.0 reduce-scatter.5.cloned.1.call-start
  298.7 32.7 %reduce-scatter.3.cloned.1.call-done = bf16[4096,1024]{1,0:T(8,128)(2,1)} async-done(((bf16[4096,2048]{1,0:T(8,128)(2,1)}), bf16[4096,1024]{1,0:T(8,128)(2,1)}) %reduce-scatter.3.cloned.1.call-update) | async-done | bytes 8388624 | tf_op jit(solution)/shard_map/reduce_scatter | solution.py:36
  331.4 0.0 reduce-scatter.5.cloned.1.call-update
  331.4 182.2 %reduce-scatter.5.cloned.1.call-done = bf16[256,1024]{1,0:T(8,128)(2,1)} async-done(((bf16[4096,1024]{1,0:T(8,128)(2,1)}), bf16[256,1024]{1,0:T(8,128)(2,1)}) %reduce-scatter.5.cloned.1.call-update) | async-done | bytes 524304 | tf_op jit(solution)/shard_map/reduce_scatter | solution.py:37
  513.6 2.3 add_convert_fusion
  (24 shorter events, 0.1 us)
Async XLA Ops:
  6.5 266.8 %copy-start = (bf16[1,512,2048]{2,1,0:T(8,128)(2,1)S(1)}, bf16[1,512,2048]{2,1,0:T(8,128)(2,1)}, u32[]{:S(2)}) copy-start(bf16[1,512,2048]{2,1,0:T(8,128)(2,1)} %param.27) | copy-start | bytes 6291460
  6.5 64.6 %all-gather.4.cloned.1.call-start = ((), (), s32[]{:S(2)}) async-start(), calls=%async_computation.2 | async-start | bytes 2228224 | tf_op jit(solution)/shard_map/all_gather | solution.py:70
  8.4 101.7 %all-reduce.2.cloned.1.call-start = ((), (), s32[]{:S(2)}) async-start(), calls=%async_computation.3 | async-start | bytes 4194304 | tf_op jit(solution)/shard_map/psum | solution.py:112
  17.2 53.9 %copy-start.8 = (s32[16]{0:T(128)S(1)}, s32[16]{0:T(128)}, u32[]{:S(2)}) copy-start(s32[16]{0:T(128)} %param.19) | copy-start | bytes 196
  17.2 53.9 %copy-start.9 = (s32[1,3]{1,0:T(1,128)S(1)}, s32[1,3]{1,0:T(1,128)}, u32[]{:S(2)}) copy-start(s32[1,3]{1,0:T(1,128)} %param.20) | copy-start | bytes 40
  79.1 2.1 copy-start.3
  82.7 1.0 copy-start.4
  83.7 26.4 %copy-start.5 = (bf16[256,2048]{1,0:T(8,128)(2,1)S(1)}, bf16[256,2048]{1,0:T(8,128)(2,1)}, u32[]{:S(2)}) copy-start(bf16[256,2048]{1,0:T(8,128)(2,1)} %param.15) | copy-start | bytes 3145732
  89.0 137.2 %all-gather.6.cloned.1.call-start = ((), (), s32[]{:S(2)}) async-start(), calls=%async_computation.4 | async-start | bytes 8912896 | tf_op jit(solution)/shard_map/all_gather | solution.py:30
  89.0 24.4 %dynamic-slice-start = ((f32[2048]{0:T(1024)}, s32[]{:T(128)}), f32[1024]{0:T(1024)S(1)}, s32[]{:S(2)}) async-start(f32[2048]{0:T(1024)} %param.22, s32[]{:T(128)} %select_n.41), calls=%async_computation.8 | async-start | bytes 8704 | tf_op jit(solution)/shard_map/dynamic_slice | solution.py:29
  112.1 1.3 copy-start.2
  114.4 143.9 %all-gather.8.cloned.1.call-start = ((), (), s32[]{:S(2)}) async-start(), calls=%async_computation.5 | async-start | bytes 25165824 | tf_op jit(solution)/shard_map/all_gather | solution.py:31
  226.2 0.7 copy-start.6
  226.2 0.7 copy-start.7
  226.2 105.1 %reduce-scatter.3.cloned.1.call-start = ((), (), s32[]{:S(2)}) async-start(), calls=%async_computation.6 | async-start | bytes 25165824 | tf_op jit(solution)/shard_map/reduce_scatter | solution.py:36
  298.6 215.0 %reduce-scatter.5.cloned.1.call-start = ((), (), s32[]{:S(2)}) async-start(), calls=%async_computation.7 | async-start | bytes 8912896 | tf_op jit(solution)/shard_map/reduce_scatter | solution.py:37
  331.4 184.6 %copy-start.1 = (bf16[1,512,2048]{2,1,0:T(8,128)(2,1)S(1)}, bf16[1,512,2048]{2,1,0:T(8,128)(2,1)}, u32[]{:S(2)}) copy-start(bf16[1,512,2048]{2,1,0:T(8,128)(2,1)} %param.27) | copy-start | bytes 6291460
Sparse Core Ops, SparseCore 0:
  10.1 60.9 all-gather.3
  89.1 20.9 all-reduce.1
  114.5 111.6 all-gather.5
  227.7 30.5 all-gather.7
  298.8 32.5 reduce-scatter.2
  333.5 180.0 reduce-scatter.4

commit v2 on v1

--- a/solution.py
+++ b/solution.py
@@ -19,22 +19,72 @@
     return flat * cap + rank
 
 
+def flip(value, bit):
+    return lax.ppermute(value, "seq", [(i, i ^ bit) for i in range(DENSE_SEQ)])
+
+
+def shift(value, step):
+    return lax.ppermute(value, "seq", [(i, (i + 4 * step) % DENSE_SEQ) for i in range(DENSE_SEQ)])
+
+
+def gather_blocks(part):
+    planes = jnp.stack([part] + [shift(part, k) for k in range(1, 4)])
+    half = part.shape[-1] // 2
+    first, second = planes[..., :half], planes[..., half:]
+    first = jnp.stack([first, flip(first, 1)], 1)
+    second = jnp.stack([second, flip(second, 2)], 1)
+    first = jnp.stack([first, flip(first, 2)], 1)
+    second = jnp.stack([second, flip(second, 1)], 2)
+    return jnp.concatenate([first, second], -1)
+
+
+def block_owners():
+    mine = lax.axis_index("seq")
+    return jnp.stack(
+        [(mine + DENSE_SEQ - 4 * k) % DENSE_SEQ ^ b for k in range(4) for b in range(4)]
+    )
+
+
+def add(a, b):
+    return (a.astype(jnp.float32) + b.astype(jnp.float32)).astype(jnp.bfloat16)
+
+
+def reduce_blocks(terms):
+    half = terms.shape[-1] // 2
+    first, second = terms[..., :half], terms[..., half:]
+    first_x = flip(first[:, :, 1], 1)
+    second_y = flip(second[:, 1], 2)
+    first = add(first[:, :, 0], first_x)
+    second = add(second[:, 0], second_y)
+    first_y = flip(first[:, 1], 2)
+    second_x = flip(second[:, 1], 1)
+    first = add(first[:, 0], first_y)
+    second = add(second[:, 0], second_x)
+    sums = []
+    for piece in (first, second):
+        arrived = [shift(piece[k], -k) for k in range(1, 4)]
+        sums.append(piece[0].astype(jnp.float32) + sum(a.astype(jnp.float32) for a in arrived))
+    return jnp.concatenate(sums, -1)
+
+
 def dense_experts(normed, expert_ids, gates, w_gate, w_up, w_down, tp_index, half):
     mine = lax.axis_index("seq")
     experts = lax.axis_size("seq")
+    rows = normed.shape[0]
     named = expert_ids[:, :, None] == jnp.arange(experts, dtype=jnp.int32)[None, None, :]
     table = jnp.sum(jnp.where(named, gates[:, :, None], 0.0), axis=1)
     table = lax.all_gather(table, "seq", axis=0, tiled=True)
     weight = lax.dynamic_slice_in_dim(table, mine, 1, 1)
+    weight = weight.reshape(experts, -1)[block_owners()].reshape(-1, 1)
     part = lax.dynamic_slice_in_dim(normed, tp_index * half, half, 1)
-    column = lax.all_gather(part, "seq", axis=0, tiled=True)
+    column = gather_blocks(part).reshape(experts * rows, half)
     tokens = lax.all_gather(column, "tp", axis=1, tiled=True)
     gate_part = jnp.dot(tokens, w_gate[0], preferred_element_type=jnp.float32)
     up_part = jnp.dot(tokens, w_up[0], preferred_element_type=jnp.float32)
     act = (jax.nn.silu(gate_part) * up_part).astype(jnp.bfloat16)
     terms = jnp.dot(act, w_down[0], preferred_element_type=jnp.float32) * weight
     terms = lax.psum_scatter(terms.astype(jnp.bfloat16), "tp", scatter_dimension=1, tiled=True)
-    return lax.psum_scatter(terms, "seq", scatter_dimension=0, tiled=True).astype(jnp.float32)
+    return reduce_blocks(terms.reshape(4, 2, 2, rows, half))
 
 
 def local(
@@ -67,14 +117,20 @@
     accum = jnp.einsum("hqk,khd->hqd", probs, own_values)
     my_nodes = path[0]
     node_ids = jnp.arange(node_len.shape[0], dtype=jnp.int32)
-    piece = lax.all_gather(prefix_kv, "seq", axis=1, tiled=True)
+    if lax.axis_size("seq") <= DENSE_SEQ:
+        owners = block_owners()
+        piece = gather_blocks(prefix_kv).transpose(3, 0, 1, 2, 4, 5)
+        piece = piece.reshape(2, -1, prefix_kv.shape[2])
+    else:
+        owners = node_ids
+        piece = lax.all_gather(prefix_kv, "seq", axis=1, tiled=True)
     start = jnp.int32(0)
     count = piece.shape[1]
 
     def absorb(state):
         best, mass, sums = state
         index = jnp.arange(count, dtype=jnp.int32)
-        node = index // SLOT
+        node = jnp.repeat(owners, SLOT)
         offset = index % SLOT
         match = node[:, None] == node_ids[None, :]
         lengths = jnp.sum(jnp.where(match, node_len[None, :], 0), axis=1)

time: 525 us -> 460 us (0.88)
  waiting for transfers between devices: 399 us -> 291 us
  starting transfers between devices: 0.21 us -> 24.7 us
  other arithmetic: 8.37 us -> 20.9 us
  local copies, waits for them, and re-layouts: 19.4 us -> 24.8 us
    ppermute x0 -> x24, waiting for transfers between devices: none -> 235 us  [the longest x12 150 us: flip(): return lax.ppermute(value, 'seq', [(i, i ^ bit) for i in range(DENSE_SEQ)])]
    reduce_scatter x1 -> x0, waiting for transfers between devices: 182 us -> none  [dense_experts(): lax.psum_scatter(terms, 'seq', scatter_dimension=0, tiled=True)]
    all_gather x2 -> x0, waiting for transfers between devices: 162 us -> none  [the longest x1 112 us: dense_experts(): column = lax.all_gather(part, 'seq', axis=0, tiled=True)]
    ppermute x0 -> x24, starting transfers between devices: none -> 24.6 us  [the longest x12 17.5 us: shift(): lax.ppermute(value, 'seq', [(i, (i + 4 * step) % DENSE_SEQ) for i in rang...]
    concatenate x0 -> x1, local copies, waits for them, and re-layouts: none -> 7.99 us  [gather_blocks(): return jnp.concatenate([first, second], -1)]
    another operation x0 -> x7, other arithmetic: none -> 6 us  [the longest x2 2.34 us: gather_blocks(): second = jnp.stack([second, flip(second, 1)], 2)]
  transfers between devices with their start and end apart: 6 -> 27, of which waited for: 6 -> 20; matrix products, arithmetic and copies ran while one was open for 2% -> 4% of each run, Pallas kernels for 0% -> 0%
where the time goes in v2:
time: 460 us; the launch traced here: 457 us
  waiting for transfers between devices  291 us (63%)
  matrix products  51.5 us (11%)
  blocking collectives  29.6 us (6%)
  local copies, waits for them, and re-layouts  24.8 us (5%)
  starting transfers between devices  24.7 us (5%)
  other arithmetic  20.9 us (5%)
  between operations  14.1 us (3%)
    ppermute x12, waiting for transfers between devices, flip(): return lax.ppermute(value, 'seq', [(i, i ^ bit) for i in range(DENSE_SEQ)])  150 us
    ppermute x12, waiting for transfers between devices, shift(): lax.ppermute(value, 'seq', [(i, (i + 4 * step) % DENSE_SEQ) for i in rang...  85.4 us
    reduce_scatter x1, waiting for transfers between devices, dense_experts(): lax.psum_scatter(terms.astype(jnp.bfloat16), 'tp', scatter_dimension=1, t...  33 us
    all_gather x1, blocking collectives, dense_experts(): table = lax.all_gather(table, 'seq', axis=0, tiled=True)  29.6 us
    dot_general x1, matrix products, dense_experts(): terms = jnp.dot(act, w_down[0], preferred_element_type=jnp.float32) * weight  25.3 us
    psum x1, waiting for transfers between devices, local(): lax.psum(partial_value, 'tp')  22.9 us
    ppermute x12, starting transfers between devices, shift(): lax.ppermute(value, 'seq', [(i, (i + 4 * step) % DENSE_SEQ) for i in rang...  17.5 us
    dot_general x1, matrix products, dense_experts(): gate_part = jnp.dot(tokens, w_gate[0], preferred_element_type=jnp.float32)  15.1 us
  transfers between devices with their start and end apart: 27, of which 20 were waited for; matrix products, arithmetic and copies ran while one was open for 4% of the time, Pallas kernels for 0%

profile of v2, /device:TPU:14, one launch (start us, length us, event | category | flops | bytes accessed | tf_op | source)
XLA Modules:
  0.0 456.5 jit_solution(9862169449973066880)
XLA Ops:
  6.5 1.6 collective-permute-start
  8.6 2.6 collective-permute-start.1
  11.2 2.2 fusion.41
  13.7 1.2 copy.68
  14.9 2.3 collective-permute-done
  17.3 2.4 collective-permute-done.1
  22.7 1.8 multiply_reduce_fusion.1
  25.9 1.2 copy.69
  27.2 2.5 collective-permute-done.5
  29.7 2.1 fusion.34
  32.3 2.0 fusion.35
  35.3 1.6 fusion.26
  36.9 7.6 %collective-permute-done.6 = bf16[4,2,2,32,512]{4,3,1,0,2:T(8,128)(2,1)} collective-permute-done((bf16[4,2,2,32,512]{4,3,1,0,2:T(8,128)(2,1)}, bf16[4,2,2,32,512]{4,3,1,0,2:T(8,128)(2,1)}, u32[]{:S(2)}, u32[]{:S(2)}) %collective-permute-start.6) | collective-permute-done | bytes 524320 | tf_op jit(solution)/shard_map/ppermute | solution.py:23
  44.6 2.3 collective-permute-done.4
  46.9 3.2 maximum_bitcast_fusion
  50.1 7.5 %conditional.1 = ((f32[8,256]{1,0:T(8,128)S(1)}, f32[8,256,128]{2,1,0:T(8,128)})) conditional(s32[]{:T(128)} %convert_element_type.102, (f32[8,256]{1,0:T(8,128)S(1)}, f32[8,256,128]{2,1,0:T(8,128)}) %tuple.12, (s32[16]{0:T(128)S(1)}, s32[16]{0:T(128)S(1)}, s32[16]{0:T(128)S(1)}, s32[1,3]{1,0:T(1,128)S(1)}, ...), branch_computations={%region_3.4_spmd, %region_4.9_spmd} | conditional | flops 547915776 | bytes 34211100 | solution.py:154
  50.4 1.7 fusion.38
  53.6 1.2 fusion.2
  54.9 1.6 fusion.7
  57.5 5.2 %convolution_bitcast_fusion = f32[256,2048]{1,0:T(8,128)} fusion(bf16[8,128,2048]{2,1,0:T(8,128)(2,1)} %bitcast.197, f32[8,256,128]{2,1,0:T(8,128)} %get-tuple-element.39, f32[8,256]{1,0:T(8,128)S(1)} %get-tuple-element.40), kind=kOutput, calls=%fused_computation.34 | convolution fusion | flops 1074266112 | bytes 7348224 | tf_op jit(solution)/shard_map/hqd,hdm->qm/dot_general | solution.py:156
  63.4 22.9 %all-reduce.2.cloned.1.call-done = f32[256,2048]{1,0:T(8,128)} async-done(((f32[256,2048]{1,0:T(8,128)}), f32[256,2048]{1,0:T(8,128)}) %all-reduce.2.cloned.1.call-update) | async-done | bytes 2097168 | tf_op jit(solution)/shard_map/psum | solution.py:168
  86.3 1.9 multiply_reduce_fusion
  88.4 1.5 collective-permute-start.7
  89.9 1.4 collective-permute-start.8
  91.4 1.5 collective-permute-start.9
  93.1 31.5 %collective-permute-done.7 = bf16[256,1024]{1,0:T(8,128)(2,1)S(1)} collective-permute-done((bf16[256,1024]{1,0:T(8,128)(2,1)S(1)}, bf16[256,1024]{1,0:T(8,128)(2,1)S(1)}, u32[]{:S(2)}, u32[]{:S(2)}) %collective-permute-start.7) | collective-permute-done | bytes 524320 | tf_op jit(solution)/shard_map/ppermute | solution.py:27
  124.5 10.8 %collective-permute-done.8 = bf16[256,1024]{1,0:T(8,128)(2,1)S(1)} collective-permute-done((bf16[256,1024]{1,0:T(8,128)(2,1)S(1)}, bf16[256,1024]{1,0:T(8,128)(2,1)S(1)}, u32[]{:S(2)}, u32[]{:S(2)}) %collective-permute-start.8) | collective-permute-done | bytes 524320 | tf_op jit(solution)/shard_map/ppermute | solution.py:27
  135.3 1.9 collective-permute-done.9
  138.8 24.2 %collective-permute-done.12 = bf16[4,256,512]{2,1,0:T(8,128)(2,1)S(1)} collective-permute-done((bf16[4,256,512]{2,1,0:T(8,128)(2,1)S(1)}, bf16[4,256,512]{2,1,0:T(8,128)(2,1)S(1)}, u32[]{:S(2)}, u32[]{:S(2)}) %collective-permute-start.12) | collective-permute-done | bytes 1048608 | tf_op jit(solution)/shard_map/ppermute | solution.py:23
  165.1 45.0 %collective-permute-done.13 = bf16[4,2,256,512]{3,2,0,1:T(8,128)(2,1)S(1)} collective-permute-done((bf16[4,2,256,512]{3,2,0,1:T(8,128)(2,1)S(1)}, bf16[4,2,256,512]{3,2,0,1:T(8,128)(2,1)S(1)}, u32[]{:S(2)}, u32[]{:S(2)}) %collective-permute-start.13) | collective-permute-done | bytes 2097184 | tf_op jit(solution)/shard_map/ppermute | solution.py:23
  210.7 4.0 maximum_maximum_fusion
  214.7 8.0 %copy.58 = bf16[4,2,2,256,1024]{4,3,2,1,0:T(8,128)(2,1)} copy(bf16[4,2,2,256,1024]{4,3,0,1,2:T(8,128)(2,1)} %maximum_maximum_fusion) | data formatting | bytes 16777216 | tf_op jit(solution)/shard_map/concatenate | solution.py:38
  223.4 29.6 %all_gather.7 = f32[4096,16]{0,1:T(8,128)S(1)} all-gather(f32[256,16]{0,1:T(8,128)S(1)} %select_reduce_fusion.1), channel_id=1, replica_groups=mesh['seq'=16,'tp'=2] {'seq'}, dimensions={0}, use_global_device_ids=true | all-gather | bytes 278528 | tf_op jit(solution)/shard_map/all_gather | solution.py:76
  253.8 15.1 %fusion.24 = f32[4096,512]{1,0:T(8,128)} fusion(bf16[4096,2048]{1,0:T(8,128)(2,1)} %all-gather.2.cloned.1.call-done, bf16[1,2048,512]{2,1,0:T(8,128)(2,1)} %param.25), kind=kOutput, calls=%fused_computation.49 | convolution fusion | flops 8589934592 | bytes 27262976 | tf_op jit(solution)/shard_map/dot_general | solution.py:82
  268.9 25.3 %multiply_convert_fusion = bf16[4096,2048]{1,0:T(8,128)(2,1)} fusion(f32[4096]{0:T(1024)S(1)} %bitcast.195, bf16[1,512,2048]{2,1,0:T(8,128)(2,1)S(1)} %copy-done, f32[4096,512]{1,0:T(8,128)} %fusion.24, bf16[4096,2048]{1,0:T(8,128)(2,1)} %all-gather.2.cloned.1.call-done, bf16[1,2048,512]{2,1,0:T(8,128)(2,1)} %param.26), kind=kOutput, calls=%fused_computation.27 | convolution fusion | flops 17209229312 | bytes 46153728 | tf_op jit(solution)/shard_map/dot_general | solution.py:85
  294.2 33.0 %reduce-scatter.2.cloned.1.call-done = bf16[4096,1024]{1,0:T(8,128)(2,1)} async-done(((bf16[4096,2048]{1,0:T(8,128)(2,1)}), bf16[4096,1024]{1,0:T(8,128)(2,1)}) %reduce-scatter.2.cloned.1.call-update) | async-done | bytes 8388624 | tf_op jit(solution)/shard_map/reduce_scatter | solution.py:86
  327.3 2.7 fusion.40
  330.8 1.2 copy-done.5
  333.3 44.7 %collective-permute-done.19 = bf16[4,2,256,512]{3,2,0,1:T(8,128)(2,1)S(1)} collective-permute-done((bf16[4,2,256,512]{3,2,0,1:T(8,128)(2,1)S(1)}, bf16[4,2,256,512]{3,2,0,1:T(8,128)(2,1)S(1)}, u32[]{:S(2)}, u32[]{:S(2)}) %collective-permute-start.19) | collective-permute-done | bytes 2097184 | tf_op jit(solution)/shard_map/ppermute | solution.py:23
  379.3 1.2 collective-permute-done.14
  381.9 21.4 %collective-permute-done.20 = bf16[4,256,512]{2,1,0:T(8,128)(2,1)S(1)} collective-permute-done((bf16[4,256,512]{2,1,0:T(8,128)(2,1)S(1)}, bf16[4,256,512]{2,1,0:T(8,128)(2,1)S(1)}, u32[]{:S(2)}, u32[]{:S(2)}) %collective-permute-start.20) | collective-permute-done | bytes 1048608 | tf_op jit(solution)/shard_map/ppermute | solution.py:23
  404.1 1.5 collective-permute-start.23
  405.7 4.2 collective-permute-start.22
  410.3 2.0 collective-permute-start.18
  412.3 10.8 %collective-permute-done.21 = bf16[256,512]{1,0:T(8,128)(2,1)S(1)} collective-permute-done((bf16[256,512]{1,0:T(8,128)(2,1)S(1)}, bf16[256,512]{1,0:T(8,128)(2,1)S(1)}, u32[]{:S(2)}, u32[]{:S(2)}) %collective-permute-start.21) | collective-permute-done | bytes 262176 | tf_op jit(solution)/shard_map/ppermute | solution.py:27
  423.2 12.7 %collective-permute-done.22 = bf16[256,512]{1,0:T(8,128)(2,1)S(1)} collective-permute-done((bf16[256,512]{1,0:T(8,128)(2,1)S(1)}, bf16[256,512]{1,0:T(8,128)(2,1)S(1)}, u32[]{:S(2)}, u32[]{:S(2)}) %collective-permute-start.22) | collective-permute-done | bytes 262176 | tf_op jit(solution)/shard_map/ppermute | solution.py:27
  436.0 10.6 %collective-permute-done.16 = bf16[256,512]{1,0:T(8,128)(2,1)S(1)} collective-permute-done((bf16[256,512]{1,0:T(8,128)(2,1)S(1)}, bf16[256,512]{1,0:T(8,128)(2,1)S(1)}, u32[]{:S(2)}, u32[]{:S(2)}) %collective-permute-start.16) | collective-permute-done | bytes 262176 | tf_op jit(solution)/shard_map/ppermute | solution.py:27
  446.6 2.3 collective-permute-done.17
  (108 shorter events, 22.8 us)
Async XLA Ops:
  6.5 262.3 %copy-start = (bf16[1,512,2048]{2,1,0:T(8,128)(2,1)S(1)}, bf16[1,512,2048]{2,1,0:T(8,128)(2,1)}, u32[]{:S(2)}) copy-start(bf16[1,512,2048]{2,1,0:T(8,128)(2,1)} %param.27) | copy-start | bytes 6291460
  6.5 13.1 %copy-start.10 = (bf16[2,32,1024]{2,1,0:T(8,128)(2,1)S(1)}, bf16[2,32,1024]{2,1,0:T(8,128)(2,1)}, u32[]{:S(2)}) copy-start(bf16[2,32,1024]{2,1,0:T(8,128)(2,1)} %param.18) | copy-start | bytes 393220
  6.5 6.9 %copy-start.9 = (bf16[256,1024]{1,0:T(8,128)(2,1)S(1)}, bf16[256,1024]{1,0:T(8,128)(2,1)}, u32[]{:S(2)}) copy-start(bf16[256,1024]{1,0:T(8,128)(2,1)} %param.16) | copy-start | bytes 1572868
  6.5 79.7 %all-reduce.2.cloned.1.call-start = ((), (), s32[]{:S(2)}) async-start(), calls=%async_computation.1 | async-start | bytes 4194304 | tf_op jit(solution)/shard_map/psum | solution.py:168
  6.5 10.7 %collective-permute-start = (bf16[2,32,1024]{2,1,0:T(8,128)(2,1)}, bf16[2,32,1024]{2,1,0:T(8,128)(2,1)S(1)}, u32[]{:S(2)}, u32[]{:S(2)}) collective-permute-start(bf16[2,32,1024]{2,1,0:T(8,128)(2,1)} %param.18), channel_id=1, source_target_pairs={{0,8},{2,10},{4,12},{6,14},{8,16},{10,18},{12,20},{14,22},{16,24},... | collective-permute-start | bytes 393224 | tf_op jit(solution)/shard_map/ppermute | solution.py:27
  8.2 9.1 %collective-permute-start.2 = (bf16[2,32,1024]{2,1,0:T(8,128)(2,1)}, bf16[2,32,1024]{2,1,0:T(8,128)(2,1)S(1)}, u32[]{:S(2)}, u32[]{:S(2)}) collective-permute-start(bf16[2,32,1024]{2,1,0:T(8,128)(2,1)} %param.18), channel_id=1, source_target_pairs={{0,24},{2,26},{4,28},{6,30},{8,0},{10,2},{12,4},{14,6},{16,8},{18,... | collective-permute-start | bytes 393224 | tf_op jit(solution)/shard_map/ppermute | solution.py:27
  8.6 11.0 %collective-permute-start.1 = (bf16[2,32,1024]{2,1,0:T(8,128)(2,1)}, bf16[2,32,1024]{2,1,0:T(8,128)(2,1)}, u32[]{:S(2)}, u32[]{:S(2)}) collective-permute-start(bf16[2,32,1024]{2,1,0:T(8,128)(2,1)} %param.18), channel_id=1, source_target_pairs={{0,16},{2,18},{4,20},{6,22},{8,24},{10,26},{12,28},{14,30},{16,0},... | collective-permute-start | bytes 393224 | tf_op jit(solution)/shard_map/ppermute | solution.py:27
  20.7 3.9 copy-start.15
  21.6 8.1 %collective-permute-start.5 = (bf16[4,2,32,512]{3,2,0,1:T(8,128)(2,1)}, bf16[4,2,32,512]{3,2,0,1:T(8,128)(2,1)}, u32[]{:S(2)}, u32[]{:S(2)}) collective-permute-start(bf16[4,2,32,512]{3,2,0,1:T(8,128)(2,1)} %get-tuple-element.93), channel_id=1, source_target_pairs={{0,4},{2,6},{4,0},{6,2},{8,12},{10,14},{12,8},{14,10},{16,20},{18,... | collective-permute-start | bytes 786440 | tf_op jit(solution)/shard_map/ppermute | solution.py:23
  22.1 10.2 %collective-permute-start.3 = (bf16[4,2,32,512]{3,2,0,1:T(8,128)(2,1)}, bf16[4,2,32,512]{3,2,0,1:T(8,128)(2,1)}, u32[]{:S(2)}, u32[]{:S(2)}) collective-permute-start(bf16[4,2,32,512]{3,2,0,1:T(8,128)(2,1)} %get-tuple-element.94), channel_id=1, source_target_pairs={{0,2},{2,0},{4,6},{6,4},{8,10},{10,8},{12,14},{14,12},{16,18},{18,... | collective-permute-start | bytes 786440 | tf_op jit(solution)/shard_map/ppermute | solution.py:23
  27.2 7.7 %copy-start.2 = (f32[8,256,256]{1,2,0:T(8,128)S(1)}, f32[8,256,256]{1,2,0:T(8,128)}, u32[]{:S(2)}) copy-start(f32[8,256,256]{1,2,0:T(8,128)} %get-tuple-element.98) | copy-start | bytes 6291460
  31.8 12.8 %collective-permute-start.6 = (bf16[4,2,2,32,512]{4,3,1,0,2:T(8,128)(2,1)}, bf16[4,2,2,32,512]{4,3,1,0,2:T(8,128)(2,1)}, u32[]{:S(2)}, u32[]{:S(2)}) collective-permute-start(bf16[4,2,2,32,512]{4,3,1,0,2:T(8,128)(2,1)} %get-tuple-element.96), channel_id=1, source_target_pairs={{0,2},{2,0},{4,6},{6,4},{8,10},{10,8},{12,14},{14,12},{16,18},{18,... | collective-permute-start | bytes 1572872 | tf_op jit(solution)/shard_map/ppermute | solution.py:23
  34.3 12.5 %collective-permute-start.4 = (bf16[4,2,2,32,512]{4,3,0,2,1:T(8,128)(2,1)}, bf16[4,2,2,32,512]{4,3,0,2,1:T(8,128)(2,1)}, u32[]{:S(2)}, u32[]{:S(2)}) collective-permute-start(bf16[4,2,2,32,512]{4,3,0,2,1:T(8,128)(2,1)} %get-tuple-element.90), channel_id=1, source_target_pairs={{0,4},{2,6},{4,0},{6,2},{8,12},{10,14},{12,8},{14,10},{16,20},{18,... | collective-permute-start | bytes 1572872 | tf_op jit(solution)/shard_map/ppermute | solution.py:23
  46.9 3.2 copy-start.14
  53.6 1.3 copy-start.6
  56.5 1.0 copy-start.7
  62.7 0.7 copy-start.13
  62.7 23.6 %copy-start.8 = (bf16[256,2048]{1,0:T(8,128)(2,1)S(1)}, bf16[256,2048]{1,0:T(8,128)(2,1)}, u32[]{:S(2)}) copy-start(bf16[256,2048]{1,0:T(8,128)(2,1)} %param.15) | copy-start | bytes 3145732
  62.7 191.1 %all-gather.2.cloned.1.call-start = ((), (), s32[]{:S(2)}) async-start(), calls=%async_computation.2 | async-start | bytes 25165824 | tf_op jit(solution)/shard_map/all_gather | solution.py:81
  88.2 4.7 %copy-start.3 = (f32[256,2048]{1,0:T(8,128)}, f32[256,2048]{1,0:T(8,128)S(1)}, u32[]{:S(2)}) copy-start(f32[256,2048]{1,0:T(8,128)S(1)} %get-tuple-element.64) | copy-start | bytes 6291460
  88.4 36.1 %collective-permute-start.7 = (bf16[256,1024]{1,0:T(8,128)(2,1)S(1)}, bf16[256,1024]{1,0:T(8,128)(2,1)S(1)}, u32[]{:S(2)}, u32[]{:S(2)}) collective-permute-start(bf16[256,1024]{1,0:T(8,128)(2,1)S(1)} %multiply_convert_fusion.2), channel_id=1, source_target_pairs={{0,8},{2,10},{4,12},{6,14},{8,16},{10,18},{12,20},{14,22},{16,24},... | collective-permute-start | bytes 1572872 | tf_op jit(solution)/shard_map/ppermute | solution.py:27
  89.9 45.3 %collective-permute-start.8 = (bf16[256,1024]{1,0:T(8,128)(2,1)S(1)}, bf16[256,1024]{1,0:T(8,128)(2,1)S(1)}, u32[]{:S(2)}, u32[]{:S(2)}) collective-permute-start(bf16[256,1024]{1,0:T(8,128)(2,1)S(1)} %multiply_convert_fusion.2), channel_id=1, source_target_pairs={{0,16},{2,18},{4,20},{6,22},{8,24},{10,26},{12,28},{14,30},{16,0},... | collective-permute-start | bytes 1572872 | tf_op jit(solution)/shard_map/ppermute | solution.py:27
  91.4 45.8 %collective-permute-start.9 = (bf16[256,1024]{1,0:T(8,128)(2,1)S(1)}, bf16[256,1024]{1,0:T(8,128)(2,1)S(1)}, u32[]{:S(2)}, u32[]{:S(2)}) collective-permute-start(bf16[256,1024]{1,0:T(8,128)(2,1)S(1)} %multiply_convert_fusion.2), channel_id=1, source_target_pairs={{0,24},{2,26},{4,28},{6,30},{8,0},{10,2},{12,4},{14,6},{16,8},{18,... | collective-permute-start | bytes 1572872 | tf_op jit(solution)/shard_map/ppermute | solution.py:27
  137.8 25.2 %collective-permute-start.12 = (bf16[4,256,512]{2,1,0:T(8,128)(2,1)S(1)}, bf16[4,256,512]{2,1,0:T(8,128)(2,1)S(1)}, u32[]{:S(2)}, u32[]{:S(2)}) collective-permute-start(bf16[4,256,512]{2,1,0:T(8,128)(2,1)S(1)} %get-tuple-element.77), channel_id=1, source_target_pairs={{0,4},{2,6},{4,0},{6,2},{8,12},{10,14},{12,8},{14,10},{16,20},{18,... | collective-permute-start | bytes 3145736 | tf_op jit(solution)/shard_map/ppermute | solution.py:23
  138.5 25.4 %collective-permute-start.10 = (bf16[4,256,512]{2,1,0:T(8,128)(2,1)S(1)}, bf16[4,256,512]{2,1,0:T(8,128)(2,1)S(1)}, u32[]{:S(2)}, u32[]{:S(2)}) collective-permute-start(bf16[4,256,512]{2,1,0:T(8,128)(2,1)S(1)} %get-tuple-element.78), channel_id=1, source_target_pairs={{0,2},{2,0},{4,6},{6,4},{8,10},{10,8},{12,14},{14,12},{16,18},{18,... | collective-permute-start | bytes 3145736 | tf_op jit(solution)/shard_map/ppermute | solution.py:23
  163.3 46.8 %collective-permute-start.13 = (bf16[4,2,256,512]{3,2,0,1:T(8,128)(2,1)S(1)}, bf16[4,2,256,512]{3,2,0,1:T(8,128)(2,1)S(1)}, u32[]{:S(2)}, u32[]{:S(2)}) collective-permute-start(bf16[4,2,256,512]{3,2,0,1:T(8,128)(2,1)S(1)} %get-tuple-element.80), channel_id=1, source_target_pairs={{0,2},{2,0},{4,6},{6,4},{8,10},{10,8},{12,14},{14,12},{16,18},{18,... | collective-permute-start | bytes 6291464 | tf_op jit(solution)/shard_map/ppermute | solution.py:23
  164.2 46.5 %collective-permute-start.11 = (bf16[4,2,256,512]{3,2,0,1:T(8,128)(2,1)S(1)}, bf16[4,2,256,512]{3,2,0,1:T(8,128)(2,1)S(1)}, u32[]{:S(2)}, u32[]{:S(2)}) collective-permute-start(bf16[4,2,256,512]{3,2,0,1:T(8,128)(2,1)S(1)} %get-tuple-element.74), channel_id=1, source_target_pairs={{0,4},{2,6},{4,0},{6,2},{8,12},{10,14},{12,8},{14,10},{16,20},{18,... | collective-permute-start | bytes 6291464 | tf_op jit(solution)/shard_map/ppermute | solution.py:23
  222.7 0.7 copy-start.11
  222.7 0.7 copy-start.12
  222.7 104.6 %reduce-scatter.2.cloned.1.call-start = ((), (), s32[]{:S(2)}) async-start(), calls=%async_computation.3 | async-start | bytes 25165824 | tf_op jit(solution)/shard_map/reduce_scatter | solution.py:86
  327.3 4.7 %copy-start.5 = (bf16[4096,1024]{1,0:T(8,128)(2,1)S(1)}, bf16[4096,1024]{1,0:T(8,128)(2,1)}, u32[]{:S(2)}) copy-start(bf16[4096,1024]{1,0:T(8,128)(2,1)} %reduce-scatter.2.cloned.1.call-done) | copy-start | bytes 25165828
  330.1 47.8 %collective-permute-start.19 = (bf16[4,2,256,512]{3,2,0,1:T(8,128)(2,1)S(1)}, bf16[4,2,256,512]{3,2,0,1:T(8,128)(2,1)S(1)}, u32[]{:S(2)}, u32[]{:S(2)}) collective-permute-start(bf16[4,2,256,512]{3,2,0,1:T(8,128)(2,1)S(1)} %bitcast.181), channel_id=1, source_target_pairs={{0,4},{2,6},{4,0},{6,2},{8,12},{10,14},{12,8},{14,10},{16,20},{18,... | collective-permute-start | bytes 6291464 | tf_op jit(solution)/shard_map/ppermute | solution.py:23
  332.7 47.8 %collective-permute-start.14 = (bf16[4,2,256,512]{3,2,0,1:T(8,128)(2,1)S(1)}, bf16[4,2,256,512]{3,2,0,1:T(8,128)(2,1)S(1)}, u32[]{:S(2)}, u32[]{:S(2)}) collective-permute-start(bf16[4,2,256,512]{3,2,0,1:T(8,128)(2,1)S(1)} %bitcast.180), channel_id=1, source_target_pairs={{0,2},{2,0},{4,6},{6,4},{8,10},{10,8},{12,14},{14,12},{16,18},{18,... | collective-permute-start | bytes 6291464 | tf_op jit(solution)/shard_map/ppermute | solution.py:23
  378.7 24.5 %collective-permute-start.20 = (bf16[4,256,512]{2,1,0:T(8,128)(2,1)S(1)}, bf16[4,256,512]{2,1,0:T(8,128)(2,1)S(1)}, u32[]{:S(2)}, u32[]{:S(2)}) collective-permute-start(bf16[4,256,512]{2,1,0:T(8,128)(2,1)S(1)} %slice_bitcast_fusion), channel_id=1, source_target_pairs={{0,2},{2,0},{4,6},{6,4},{8,10},{10,8},{12,14},{14,12},{16,18},{18,... | collective-permute-start | bytes 3145736 | tf_op jit(solution)/shard_map/ppermute | solution.py:23
  381.2 28.7 %collective-permute-start.15 = (bf16[4,256,512]{2,1,0:T(8,128)(2,1)S(1)}, bf16[4,256,512]{2,1,0:T(8,128)(2,1)S(1)}, u32[]{:S(2)}, u32[]{:S(2)}) collective-permute-start(bf16[4,256,512]{2,1,0:T(8,128)(2,1)S(1)} %slice_bitcast_fusion.2), channel_id=1, source_target_pairs={{0,4},{2,6},{4,0},{6,2},{8,12},{10,14},{12,8},{14,10},{16,20},{18,... | collective-permute-start | bytes 3145736 | tf_op jit(solution)/shard_map/ppermute | solution.py:23
  403.6 19.6 %collective-permute-start.21 = (bf16[256,512]{1,0:T(8,128)(2,1)S(1)}, bf16[256,512]{1,0:T(8,128)(2,1)S(1)}, u32[]{:S(2)}, u32[]{:S(2)}) collective-permute-start(bf16[256,512]{1,0:T(8,128)(2,1)S(1)} %get-tuple-element.84), channel_id=1, source_target_pairs={{0,24},{2,26},{4,28},{6,30},{8,0},{10,2},{12,4},{14,6},{16,8},{18,... | collective-permute-start | bytes 786440 | tf_op jit(solution)/shard_map/ppermute | solution.py:27
  404.1 19.0 %collective-permute-start.23 = (bf16[256,512]{1,0:T(8,128)(2,1)S(1)}, bf16[256,512]{1,0:T(8,128)(2,1)S(1)}, u32[]{:S(2)}, u32[]{:S(2)}) collective-permute-start(bf16[256,512]{1,0:T(8,128)(2,1)S(1)} %get-tuple-element.85), channel_id=1, source_target_pairs={{0,8},{2,10},{4,12},{6,14},{8,16},{10,18},{12,20},{14,22},{16,24},... | collective-permute-start | bytes 786440 | tf_op jit(solution)/shard_map/ppermute | solution.py:27
  405.7 30.2 %collective-permute-start.22 = (bf16[256,512]{1,0:T(8,128)(2,1)S(1)}, bf16[256,512]{1,0:T(8,128)(2,1)S(1)}, u32[]{:S(2)}, u32[]{:S(2)}) collective-permute-start(bf16[256,512]{1,0:T(8,128)(2,1)S(1)} %get-tuple-element.86), channel_id=1, source_target_pairs={{0,16},{2,18},{4,20},{6,22},{8,24},{10,26},{12,28},{14,30},{16,0},... | collective-permute-start | bytes 786440 | tf_op jit(solution)/shard_map/ppermute | solution.py:27
  410.2 38.9 %copy-start.4 = (f32[256,2048]{1,0:T(8,128)S(1)}, f32[256,2048]{1,0:T(8,128)}, u32[]{:S(2)}) copy-start(f32[256,2048]{1,0:T(8,128)} %copy-done.3) | copy-start | bytes 6291460
  410.3 36.3 %collective-permute-start.16 = (bf16[256,512]{1,0:T(8,128)(2,1)S(1)}, bf16[256,512]{1,0:T(8,128)(2,1)S(1)}, u32[]{:S(2)}, u32[]{:S(2)}) collective-permute-start(bf16[256,512]{1,0:T(8,128)(2,1)S(1)} %get-tuple-element.81), channel_id=1, source_target_pairs={{0,24},{2,26},{4,28},{6,30},{8,0},{10,2},{12,4},{14,6},{16,8},{18,... | collective-permute-start | bytes 786440 | tf_op jit(solution)/shard_map/ppermute | solution.py:27
  410.3 36.3 %collective-permute-start.18 = (bf16[256,512]{1,0:T(8,128)(2,1)S(1)}, bf16[256,512]{1,0:T(8,128)(2,1)S(1)}, u32[]{:S(2)}, u32[]{:S(2)}) collective-permute-start(bf16[256,512]{1,0:T(8,128)(2,1)S(1)} %get-tuple-element.82), channel_id=1, source_target_pairs={{0,8},{2,10},{4,12},{6,14},{8,16},{10,18},{12,20},{14,22},{16,24},... | collective-permute-start | bytes 786440 | tf_op jit(solution)/shard_map/ppermute | solution.py:27
  423.2 25.8 %collective-permute-start.17 = (bf16[256,512]{1,0:T(8,128)(2,1)S(1)}, bf16[256,512]{1,0:T(8,128)(2,1)S(1)}, u32[]{:S(2)}, u32[]{:S(2)}) collective-permute-start(bf16[256,512]{1,0:T(8,128)(2,1)S(1)} %get-tuple-element.83), channel_id=1, source_target_pairs={{0,16},{2,18},{4,20},{6,22},{8,24},{10,26},{12,28},{14,30},{16,0},... | collective-permute-start | bytes 786440 | tf_op jit(solution)/shard_map/ppermute | solution.py:27
  435.9 14.1 %copy-start.1 = (bf16[1,512,2048]{2,1,0:T(8,128)(2,1)S(1)}, bf16[1,512,2048]{2,1,0:T(8,128)(2,1)}, u32[]{:S(2)}) copy-start(bf16[1,512,2048]{2,1,0:T(8,128)(2,1)} %param.27) | copy-start | bytes 6291460
Sparse Core Ops, SparseCore 0:
  62.8 23.3 all-reduce.1
  222.8 29.3 all-gather.1
  294.3 32.8 reduce-scatter.1

commit v3 on v2

--- a/solution.py
+++ b/solution.py
@@ -78,9 +78,12 @@
     weight = weight.reshape(experts, -1)[block_owners()].reshape(-1, 1)
     part = lax.dynamic_slice_in_dim(normed, tp_index * half, half, 1)
     column = gather_blocks(part).reshape(experts * rows, half)
-    tokens = lax.all_gather(column, "tp", axis=1, tiled=True)
-    gate_part = jnp.dot(tokens, w_gate[0], preferred_element_type=jnp.float32)
-    up_part = jnp.dot(tokens, w_up[0], preferred_element_type=jnp.float32)
+    other = lax.ppermute(column, "tp", [(0, 1), (1, 0)])
+    tokens = jnp.concatenate([column, other], 1)
+    w_gate = jnp.where(tp_index == 0, w_gate[0], jnp.roll(w_gate[0], half, 0))
+    w_up = jnp.where(tp_index == 0, w_up[0], jnp.roll(w_up[0], half, 0))
+    gate_part = jnp.dot(tokens, w_gate, preferred_element_type=jnp.float32)
+    up_part = jnp.dot(tokens, w_up, preferred_element_type=jnp.float32)
     act = (jax.nn.silu(gate_part) * up_part).astype(jnp.bfloat16)
     terms = jnp.dot(act, w_down[0], preferred_element_type=jnp.float32) * weight
     terms = lax.psum_scatter(terms.astype(jnp.bfloat16), "tp", scatter_dimension=1, tiled=True)

time: 460 us -> 473 us (1.028)
  matrix products: 51.5 us -> 58 us
  local copies, waits for them, and re-layouts: 24.8 us -> 30.5 us
    dot_general x1 -> x2, matrix products: 15.1 us -> 30.3 us  [the longest x1 15.2 us: dense_experts(): gate_part = jnp.dot(tokens, w_gate, preferred_element_type=jnp.float32)]
    dot_general x1, matrix products: 25.3 us -> 16.5 us  [dense_experts(): terms = jnp.dot(act, w_down[0], preferred_element_type=jnp.float32) * weight]
  transfers between devices with their start and end apart: 27 -> 27, of which waited for: 20 -> 22; matrix products, arithmetic and copies ran while one was open for 4% -> 5% of each run, Pallas kernels for 0% -> 0%
where the time goes in v3:
time: 473 us; the launch traced here: 470 us
  waiting for transfers between devices  294 us (62%)
  matrix products  58 us (12%)
  local copies, waits for them, and re-layouts  30.5 us (6%)
  blocking collectives  29.4 us (6%)
  starting transfers between devices  23.1 us (5%)
  other arithmetic  20.9 us (4%)
  between operations  14.3 us (3%)
    ppermute x12, waiting for transfers between devices, flip(): return lax.ppermute(value, 'seq', [(i, i ^ bit) for i in range(DENSE_SEQ)])  151 us
    ppermute x12, waiting for transfers between devices, shift(): lax.ppermute(value, 'seq', [(i, (i + 4 * step) % DENSE_SEQ) for i in rang...  89.8 us
    reduce_scatter x1, waiting for transfers between devices, dense_experts(): lax.psum_scatter(terms.astype(jnp.bfloat16), 'tp', scatter_dimension=1, t...  33.1 us
    all_gather x1, blocking collectives, dense_experts(): table = lax.all_gather(table, 'seq', axis=0, tiled=True)  29.4 us
    psum x1, waiting for transfers between devices, local(): lax.psum(partial_value, 'tp')  20.1 us
    dot_general x1, matrix products, dense_experts(): terms = jnp.dot(act, w_down[0], preferred_element_type=jnp.float32) * weight  16.5 us
    ppermute x12, starting transfers between devices, shift(): lax.ppermute(value, 'seq', [(i, (i + 4 * step) % DENSE_SEQ) for i in rang...  16 us
    dot_general x1, matrix products, dense_experts(): gate_part = jnp.dot(tokens, w_gate, preferred_element_type=jnp.float32)  15.2 us
  transfers between devices with their start and end apart: 27, of which 22 were waited for; matrix products, arithmetic and copies ran while one was open for 5% of the time, Pallas kernels for 0%

profile of v3, /device:TPU:14, one launch (start us, length us, event | category | flops | bytes accessed | tf_op | source)
XLA Modules:
  0.0 469.9 jit_solution(10815425243909460726)
XLA Ops:
  6.5 1.6 collective-permute-start
  9.4 1.8 collective-permute-start.2
  11.2 2.1 fusion.52
  14.7 3.3 collective-permute-done
  18.0 1.7 collective-permute-done.1
  19.6 1.8 collective-permute-done.2
  24.4 1.8 multiply_reduce_fusion.1
  28.8 3.1 collective-permute-done.3
  31.9 2.1 fusion.46
  34.5 2.0 fusion.45
  37.3 1.6 fusion.34
  39.0 8.2 %collective-permute-done.4 = bf16[4,2,2,32,512]{4,3,0,2,1:T(8,128)(2,1)} collective-permute-done((bf16[4,2,2,32,512]{4,3,0,2,1:T(8,128)(2,1)}, bf16[4,2,2,32,512]{4,3,0,2,1:T(8,128)(2,1)}, u32[]{:S(2)}, u32[]{:S(2)}) %collective-permute-start.4) | collective-permute-done | bytes 524320 | tf_op jit(solution)/shard_map/ppermute | solution.py:23
  47.3 2.2 collective-permute-done.6
  49.5 3.2 maximum_bitcast_fusion
  52.7 8.4 %conditional.1 = ((f32[8,256]{1,0:T(8,128)S(1)}, f32[8,256,128]{2,1,0:T(8,128)})) conditional(s32[]{:T(128)} %convert_element_type.102, (f32[8,256]{1,0:T(8,128)S(1)}, f32[8,256,128]{2,1,0:T(8,128)}) %tuple.12, (s32[16]{0:T(128)S(1)}, s32[16]{0:T(128)S(1)}, s32[16]{0:T(128)S(1)}, s32[1,3]{1,0:T(1,128)S(1)}, ...), branch_computations={%region_3.4_spmd, %region_4.9_spmd} | conditional | flops 547915776 | bytes 34211100 | solution.py:157
  53.0 1.7 fusion.49
  58.5 1.6 fusion.7
  61.1 5.2 %convolution_bitcast_fusion = f32[256,2048]{1,0:T(8,128)} fusion(bf16[8,128,2048]{2,1,0:T(8,128)(2,1)} %bitcast.200, f32[8,256,128]{2,1,0:T(8,128)} %get-tuple-element.39, f32[8,256]{1,0:T(8,128)S(1)} %get-tuple-element.40), kind=kOutput, calls=%fused_computation.38 | convolution fusion | flops 1074266112 | bytes 7348224 | tf_op jit(solution)/shard_map/hqd,hdm->qm/dot_general | solution.py:159
  67.0 20.1 %all-reduce.2.cloned.1.call-done = f32[256,2048]{1,0:T(8,128)} async-done(((f32[256,2048]{1,0:T(8,128)}), f32[256,2048]{1,0:T(8,128)}) %all-reduce.2.cloned.1.call-update) | async-done | bytes 2097168 | tf_op jit(solution)/shard_map/psum | solution.py:171
  87.0 1.9 multiply_reduce_fusion
  89.2 1.5 collective-permute-start.7
  90.7 1.4 collective-permute-start.8
  92.1 1.5 collective-permute-start.9
  93.8 31.5 %collective-permute-done.7 = bf16[256,1024]{1,0:T(8,128)(2,1)S(1)} collective-permute-done((bf16[256,1024]{1,0:T(8,128)(2,1)S(1)}, bf16[256,1024]{1,0:T(8,128)(2,1)S(1)}, u32[]{:S(2)}, u32[]{:S(2)}) %collective-permute-start.7) | collective-permute-done | bytes 524320 | tf_op jit(solution)/shard_map/ppermute | solution.py:27
  125.3 10.8 %collective-permute-done.8 = bf16[256,1024]{1,0:T(8,128)(2,1)S(1)} collective-permute-done((bf16[256,1024]{1,0:T(8,128)(2,1)S(1)}, bf16[256,1024]{1,0:T(8,128)(2,1)S(1)}, u32[]{:S(2)}, u32[]{:S(2)}) %collective-permute-start.8) | collective-permute-done | bytes 524320 | tf_op jit(solution)/shard_map/ppermute | solution.py:27
  136.0 1.9 collective-permute-done.9
  139.6 24.2 %collective-permute-done.10 = bf16[4,256,512]{2,1,0:T(8,128)(2,1)S(1)} collective-permute-done((bf16[4,256,512]{2,1,0:T(8,128)(2,1)S(1)}, bf16[4,256,512]{2,1,0:T(8,128)(2,1)S(1)}, u32[]{:S(2)}, u32[]{:S(2)}) %collective-permute-start.10) | collective-permute-done | bytes 1048608 | tf_op jit(solution)/shard_map/ppermute | solution.py:23
  165.8 45.0 %collective-permute-done.11 = bf16[4,2,256,512]{3,2,0,1:T(8,128)(2,1)S(1)} collective-permute-done((bf16[4,2,256,512]{3,2,0,1:T(8,128)(2,1)S(1)}, bf16[4,2,256,512]{3,2,0,1:T(8,128)(2,1)S(1)}, u32[]{:S(2)}, u32[]{:S(2)}) %collective-permute-start.11) | collective-permute-done | bytes 2097184 | tf_op jit(solution)/shard_map/ppermute | solution.py:23
  211.4 4.0 maximum_maximum_fusion
  215.4 8.0 %copy.58 = bf16[4,2,2,256,1024]{4,3,2,1,0:T(8,128)(2,1)} copy(bf16[4,2,2,256,1024]{4,3,0,1,2:T(8,128)(2,1)} %maximum_maximum_fusion) | data formatting | bytes 16777216 | tf_op jit(solution)/shard_map/concatenate | solution.py:38
  223.5 29.4 %all_gather.3 = f32[4096,16]{0,1:T(8,128)S(1)} all-gather(f32[256,16]{0,1:T(8,128)S(1)} %select_reduce_fusion.1), channel_id=1, replica_groups=mesh['seq'=16,'tp'=2] {'seq'}, dimensions={0}, use_global_device_ids=true | all-gather | bytes 278528 | tf_op jit(solution)/shard_map/all_gather | solution.py:76
  253.7 3.2 slice_bitcast_fusion.7
  256.9 1.5 slice_bitcast_fusion.5
  259.2 15.2 %fusion.19 = f32[4096,512]{1,0:T(8,128)} fusion(bf16[4096,1024]{1,0:T(8,128)(2,1)} %collective-permute-done.14, bf16[4096,1024]{1,0:T(8,128)(2,1)} %bitcast.173, bf16[1024,512]{1,0:T(8,128)(2,1)} %get-tuple-element.74, bf16[1024,512]{1,0:T(8,128)(2,1)} %get-tuple-element.73, bf16[1,2048,512]{2,1,0:T(8,128)(2,1)S(1)} %copy-done.5, pred[]{:T(512)S(6)} %eq.82), kind=kOutput, calls=%fused_computation.30 | convolution fusion | flops 8628731904 | bytes 29360128 | tf_op jit(solution)/shard_map/dot_general | solution.py:85
  274.4 15.1 %fusion.18 = f32[4096,512]{1,0:T(8,128)} fusion(bf16[4096,1024]{1,0:T(8,128)(2,1)} %collective-permute-done.14, bf16[4096,1024]{1,0:T(8,128)(2,1)} %bitcast.174, bf16[1024,512]{1,0:T(8,128)(2,1)} %get-tuple-element.76, bf16[1024,512]{1,0:T(8,128)(2,1)} %get-tuple-element.75, bf16[1,2048,512]{2,1,0:T(8,128)(2,1)S(1)} %copy-done.6, pred[]{:T(512)S(6)} %eq.82), kind=kOutput, calls=%fused_computation.29 | convolution fusion | flops 8628731904 | bytes 29360128 | tf_op jit(solution)/shard_map/dot_general | solution.py:86
  289.6 16.5 %multiply_convert_fusion = bf16[4096,2048]{1,0:T(8,128)(2,1)} fusion(f32[4096]{0:T(1024)S(1)} %bitcast.198, f32[4096,512]{1,0:T(8,128)} %fusion.18, f32[4096,512]{1,0:T(8,128)} %fusion.19, bf16[1,512,2048]{2,1,0:T(8,128)(2,1)S(1)} %copy-done), kind=kOutput, calls=%fused_computation.27 | convolution fusion | flops 8619294720 | bytes 35667968 | tf_op jit(solution)/shard_map/dot_general | solution.py:88
  306.1 33.1 %reduce-scatter.2.cloned.1.call-done = bf16[4096,1024]{1,0:T(8,128)(2,1)} async-done(((bf16[4096,2048]{1,0:T(8,128)(2,1)}), bf16[4096,1024]{1,0:T(8,128)(2,1)}) %reduce-scatter.2.cloned.1.call-update) | async-done | bytes 8388624 | tf_op jit(solution)/shard_map/reduce_scatter | solution.py:89
  339.2 2.7 fusion.50
  345.2 44.7 %collective-permute-done.15 = bf16[4,2,256,512]{3,2,0,1:T(8,128)(2,1)S(1)} collective-permute-done((bf16[4,2,256,512]{3,2,0,1:T(8,128)(2,1)S(1)}, bf16[4,2,256,512]{3,2,0,1:T(8,128)(2,1)S(1)}, u32[]{:S(2)}, u32[]{:S(2)}) %collective-permute-start.15) | collective-permute-done | bytes 2097184 | tf_op jit(solution)/shard_map/ppermute | solution.py:23
  393.8 21.4 %collective-permute-done.16 = bf16[4,256,512]{2,1,0:T(8,128)(2,1)S(1)} collective-permute-done((bf16[4,256,512]{2,1,0:T(8,128)(2,1)S(1)}, bf16[4,256,512]{2,1,0:T(8,128)(2,1)S(1)}, u32[]{:S(2)}, u32[]{:S(2)}) %collective-permute-start.16) | collective-permute-done | bytes 1048608 | tf_op jit(solution)/shard_map/ppermute | solution.py:23
  416.2 2.4 collective-permute-start.18
  418.6 2.3 collective-permute-start.19
  421.4 1.5 collective-permute-start.23
  422.9 12.2 %collective-permute-done.17 = bf16[256,512]{1,0:T(8,128)(2,1)S(1)} collective-permute-done((bf16[256,512]{1,0:T(8,128)(2,1)S(1)}, bf16[256,512]{1,0:T(8,128)(2,1)S(1)}, u32[]{:S(2)}, u32[]{:S(2)}) %collective-permute-start.17) | collective-permute-done | bytes 262176 | tf_op jit(solution)/shard_map/ppermute | solution.py:27
  435.1 1.7 collective-permute-done.18
  436.8 14.7 %collective-permute-done.19 = bf16[256,512]{1,0:T(8,128)(2,1)S(1)} collective-permute-done((bf16[256,512]{1,0:T(8,128)(2,1)S(1)}, bf16[256,512]{1,0:T(8,128)(2,1)S(1)}, u32[]{:S(2)}, u32[]{:S(2)}) %collective-permute-start.19) | collective-permute-done | bytes 262176 | tf_op jit(solution)/shard_map/ppermute | solution.py:27
  451.6 6.9 %collective-permute-done.22 = bf16[256,512]{1,0:T(8,128)(2,1)S(1)} collective-permute-done((bf16[256,512]{1,0:T(8,128)(2,1)S(1)}, bf16[256,512]{1,0:T(8,128)(2,1)S(1)}, u32[]{:S(2)}, u32[]{:S(2)}) %collective-permute-start.22) | collective-permute-done | bytes 262176 | tf_op jit(solution)/shard_map/ppermute | solution.py:27
  458.6 3.4 collective-permute-done.24
  (110 shorter events, 30.8 us)
Async XLA Ops:
  6.5 283.0 %copy-start = (bf16[1,512,2048]{2,1,0:T(8,128)(2,1)S(1)}, bf16[1,512,2048]{2,1,0:T(8,128)(2,1)}, u32[]{:S(2)}) copy-start(bf16[1,512,2048]{2,1,0:T(8,128)(2,1)} %param.27) | copy-start | bytes 6291460
  6.5 14.9 %copy-start.10 = (bf16[2,32,1024]{2,1,0:T(8,128)(2,1)S(1)}, bf16[2,32,1024]{2,1,0:T(8,128)(2,1)}, u32[]{:S(2)}) copy-start(bf16[2,32,1024]{2,1,0:T(8,128)(2,1)} %param.18) | copy-start | bytes 393220
  6.5 80.5 %all-reduce.2.cloned.1.call-start = ((), (), s32[]{:S(2)}) async-start(), calls=%async_computation.1 | async-start | bytes 4194304 | tf_op jit(solution)/shard_map/psum | solution.py:171
  6.5 11.4 %collective-permute-start = (bf16[2,32,1024]{2,1,0:T(8,128)(2,1)}, bf16[2,32,1024]{2,1,0:T(8,128)(2,1)S(1)}, u32[]{:S(2)}, u32[]{:S(2)}) collective-permute-start(bf16[2,32,1024]{2,1,0:T(8,128)(2,1)} %param.18), channel_id=1, source_target_pairs={{0,8},{2,10},{4,12},{6,14},{8,16},{10,18},{12,20},{14,22},{16,24},... | collective-permute-start | bytes 393224 | tf_op jit(solution)/shard_map/ppermute | solution.py:27
  8.1 11.5 %collective-permute-start.1 = (bf16[2,32,1024]{2,1,0:T(8,128)(2,1)}, bf16[2,32,1024]{2,1,0:T(8,128)(2,1)S(1)}, u32[]{:S(2)}, u32[]{:S(2)}) collective-permute-start(bf16[2,32,1024]{2,1,0:T(8,128)(2,1)} %param.18), channel_id=1, source_target_pairs={{0,16},{2,18},{4,20},{6,22},{8,24},{10,26},{12,28},{14,30},{16,0},... | collective-permute-start | bytes 393224 | tf_op jit(solution)/shard_map/ppermute | solution.py:27
  9.4 12.0 %collective-permute-start.2 = (bf16[2,32,1024]{2,1,0:T(8,128)(2,1)}, bf16[2,32,1024]{2,1,0:T(8,128)(2,1)}, u32[]{:S(2)}, u32[]{:S(2)}) collective-permute-start(bf16[2,32,1024]{2,1,0:T(8,128)(2,1)} %param.18), channel_id=1, source_target_pairs={{0,24},{2,26},{4,28},{6,30},{8,0},{10,2},{12,4},{14,6},{16,8},{18,... | collective-permute-start | bytes 393224 | tf_op jit(solution)/shard_map/ppermute | solution.py:27
  23.3 8.5 %collective-permute-start.3 = (bf16[4,2,32,512]{3,2,0,1:T(8,128)(2,1)}, bf16[4,2,32,512]{3,2,0,1:T(8,128)(2,1)}, u32[]{:S(2)}, u32[]{:S(2)}) collective-permute-start(bf16[4,2,32,512]{3,2,0,1:T(8,128)(2,1)} %get-tuple-element.98), channel_id=1, source_target_pairs={{0,2},{2,0},{4,6},{6,4},{8,10},{10,8},{12,14},{14,12},{16,18},{18,... | collective-permute-start | bytes 786440 | tf_op jit(solution)/shard_map/ppermute | solution.py:23
  23.9 10.6 %collective-permute-start.5 = (bf16[4,2,32,512]{3,2,0,1:T(8,128)(2,1)}, bf16[4,2,32,512]{3,2,0,1:T(8,128)(2,1)}, u32[]{:S(2)}, u32[]{:S(2)}) collective-permute-start(bf16[4,2,32,512]{3,2,0,1:T(8,128)(2,1)} %get-tuple-element.97), channel_id=1, source_target_pairs={{0,4},{2,6},{4,0},{6,2},{8,12},{10,14},{12,8},{14,10},{16,20},{18,... | collective-permute-start | bytes 786440 | tf_op jit(solution)/shard_map/ppermute | solution.py:23
  24.4 3.1 copy-start.15
  28.8 8.2 %copy-start.1 = (f32[8,256,256]{1,2,0:T(8,128)S(1)}, f32[8,256,256]{1,2,0:T(8,128)}, u32[]{:S(2)}) copy-start(f32[8,256,256]{1,2,0:T(8,128)} %get-tuple-element.102) | copy-start | bytes 6291460
  33.9 13.3 %collective-permute-start.4 = (bf16[4,2,2,32,512]{4,3,0,2,1:T(8,128)(2,1)}, bf16[4,2,2,32,512]{4,3,0,2,1:T(8,128)(2,1)}, u32[]{:S(2)}, u32[]{:S(2)}) collective-permute-start(bf16[4,2,2,32,512]{4,3,0,2,1:T(8,128)(2,1)} %get-tuple-element.94), channel_id=1, source_target_pairs={{0,4},{2,6},{4,0},{6,2},{8,12},{10,14},{12,8},{14,10},{16,20},{18,... | collective-permute-start | bytes 1572872 | tf_op jit(solution)/shard_map/ppermute | solution.py:23
  36.4 13.0 %collective-permute-start.6 = (bf16[4,2,2,32,512]{4,3,1,0,2:T(8,128)(2,1)}, bf16[4,2,2,32,512]{4,3,1,0,2:T(8,128)(2,1)}, u32[]{:S(2)}, u32[]{:S(2)}) collective-permute-start(bf16[4,2,2,32,512]{4,3,1,0,2:T(8,128)(2,1)} %get-tuple-element.100), channel_id=1, source_target_pairs={{0,2},{2,0},{4,6},{6,4},{8,10},{10,8},{12,14},{14,12},{16,18},{18,... | collective-permute-start | bytes 1572872 | tf_op jit(solution)/shard_map/ppermute | solution.py:23
  49.5 3.2 copy-start.14
  57.2 1.2 copy-start.7
  60.1 1.0 copy-start.8
  66.3 0.7 copy-start.13
  66.3 20.8 %copy-start.9 = (bf16[256,2048]{1,0:T(8,128)(2,1)S(1)}, bf16[256,2048]{1,0:T(8,128)(2,1)}, u32[]{:S(2)}) copy-start(bf16[256,2048]{1,0:T(8,128)(2,1)} %param.15) | copy-start | bytes 3145732
  66.3 272.9 %reduce-scatter.2.cloned.1.call-start = ((), (), s32[]{:S(2)}) async-start(), calls=%async_computation.2 | async-start | bytes 25165824 | tf_op jit(solution)/shard_map/reduce_scatter | solution.py:89
  89.0 4.7 copy-start.2
  89.2 36.1 %collective-permute-start.7 = (bf16[256,1024]{1,0:T(8,128)(2,1)S(1)}, bf16[256,1024]{1,0:T(8,128)(2,1)S(1)}, u32[]{:S(2)}, u32[]{:S(2)}) collective-permute-start(bf16[256,1024]{1,0:T(8,128)(2,1)S(1)} %multiply_convert_fusion.3), channel_id=1, source_target_pairs={{0,8},{2,10},{4,12},{6,14},{8,16},{10,18},{12,20},{14,22},{16,24},... | collective-permute-start | bytes 1572872 | tf_op jit(solution)/shard_map/ppermute | solution.py:27
  90.7 45.3 %collective-permute-start.8 = (bf16[256,1024]{1,0:T(8,128)(2,1)S(1)}, bf16[256,1024]{1,0:T(8,128)(2,1)S(1)}, u32[]{:S(2)}, u32[]{:S(2)}) collective-permute-start(bf16[256,1024]{1,0:T(8,128)(2,1)S(1)} %multiply_convert_fusion.3), channel_id=1, source_target_pairs={{0,16},{2,18},{4,20},{6,22},{8,24},{10,26},{12,28},{14,30},{16,0},... | collective-permute-start | bytes 1572872 | tf_op jit(solution)/shard_map/ppermute | solution.py:27
  92.1 45.8 %collective-permute-start.9 = (bf16[256,1024]{1,0:T(8,128)(2,1)S(1)}, bf16[256,1024]{1,0:T(8,128)(2,1)S(1)}, u32[]{:S(2)}, u32[]{:S(2)}) collective-permute-start(bf16[256,1024]{1,0:T(8,128)(2,1)S(1)} %multiply_convert_fusion.3), channel_id=1, source_target_pairs={{0,24},{2,26},{4,28},{6,30},{8,0},{10,2},{12,4},{14,6},{16,8},{18,... | collective-permute-start | bytes 1572872 | tf_op jit(solution)/shard_map/ppermute | solution.py:27
  138.6 25.2 %collective-permute-start.10 = (bf16[4,256,512]{2,1,0:T(8,128)(2,1)S(1)}, bf16[4,256,512]{2,1,0:T(8,128)(2,1)S(1)}, u32[]{:S(2)}, u32[]{:S(2)}) collective-permute-start(bf16[4,256,512]{2,1,0:T(8,128)(2,1)S(1)} %get-tuple-element.82), channel_id=1, source_target_pairs={{0,2},{2,0},{4,6},{6,4},{8,10},{10,8},{12,14},{14,12},{16,18},{18,... | collective-permute-start | bytes 3145736 | tf_op jit(solution)/shard_map/ppermute | solution.py:23
  139.2 25.4 %collective-permute-start.12 = (bf16[4,256,512]{2,1,0:T(8,128)(2,1)S(1)}, bf16[4,256,512]{2,1,0:T(8,128)(2,1)S(1)}, u32[]{:S(2)}, u32[]{:S(2)}) collective-permute-start(bf16[4,256,512]{2,1,0:T(8,128)(2,1)S(1)} %get-tuple-element.81), channel_id=1, source_target_pairs={{0,4},{2,6},{4,0},{6,2},{8,12},{10,14},{12,8},{14,10},{16,20},{18,... | collective-permute-start | bytes 3145736 | tf_op jit(solution)/shard_map/ppermute | solution.py:23
  164.0 46.8 %collective-permute-start.11 = (bf16[4,2,256,512]{3,2,0,1:T(8,128)(2,1)S(1)}, bf16[4,2,256,512]{3,2,0,1:T(8,128)(2,1)S(1)}, u32[]{:S(2)}, u32[]{:S(2)}) collective-permute-start(bf16[4,2,256,512]{3,2,0,1:T(8,128)(2,1)S(1)} %get-tuple-element.78), channel_id=1, source_target_pairs={{0,4},{2,6},{4,0},{6,2},{8,12},{10,14},{12,8},{14,10},{16,20},{18,... | collective-permute-start | bytes 6291464 | tf_op jit(solution)/shard_map/ppermute | solution.py:23
  164.9 46.5 %collective-permute-start.13 = (bf16[4,2,256,512]{3,2,0,1:T(8,128)(2,1)S(1)}, bf16[4,2,256,512]{3,2,0,1:T(8,128)(2,1)S(1)}, u32[]{:S(2)}, u32[]{:S(2)}) collective-permute-start(bf16[4,2,256,512]{3,2,0,1:T(8,128)(2,1)S(1)} %get-tuple-element.84), channel_id=1, source_target_pairs={{0,2},{2,0},{4,6},{6,4},{8,10},{10,8},{12,14},{14,12},{16,18},{18,... | collective-permute-start | bytes 6291464 | tf_op jit(solution)/shard_map/ppermute | solution.py:23
  215.4 8.0 %copy-start.11 = (f32[256,8]{0,1:T(8,128)S(1)}, f32[256,8]{0,1:T(8,128)}, u32[]{:S(2)}) copy-start(f32[256,8]{0,1:T(8,128)} %param.24) | copy-start | bytes 24580
  215.4 8.0 %copy-start.12 = (s32[256,8]{0,1:T(8,128)S(1)}, s32[256,8]{0,1:T(8,128)}, u32[]{:S(2)}) copy-start(s32[256,8]{0,1:T(8,128)} %param.23) | copy-start | bytes 24580
  223.4 35.0 %collective-permute-start.14 = (bf16[4096,1024]{1,0:T(8,128)(2,1)}, bf16[4096,1024]{1,0:T(8,128)(2,1)}, u32[]{:S(2)}, u32[]{:S(2)}) collective-permute-start(bf16[4096,1024]{1,0:T(8,128)(2,1)} %bitcast.172), channel_id=1, source_target_pairs={{0,1},{1,0},{2,3},{3,2},{4,5},{5,4},{6,7},{7,6},{8,9},{9,8},{10,11... | collective-permute-start | bytes 25165832 | tf_op jit(solution)/shard_map/ppermute | solution.py:81
  253.7 3.2 copy-start.6
  256.9 2.3 copy-start.5
  339.2 4.7 copy-start.4
  342.1 47.8 %collective-permute-start.15 = (bf16[4,2,256,512]{3,2,0,1:T(8,128)(2,1)S(1)}, bf16[4,2,256,512]{3,2,0,1:T(8,128)(2,1)S(1)}, u32[]{:S(2)}, u32[]{:S(2)}) collective-permute-start(bf16[4,2,256,512]{3,2,0,1:T(8,128)(2,1)S(1)} %bitcast.184), channel_id=1, source_target_pairs={{0,2},{2,0},{4,6},{6,4},{8,10},{10,8},{12,14},{14,12},{16,18},{18,... | collective-permute-start | bytes 6291464 | tf_op jit(solution)/shard_map/ppermute | solution.py:23
  344.6 47.8 %collective-permute-start.20 = (bf16[4,2,256,512]{3,2,0,1:T(8,128)(2,1)S(1)}, bf16[4,2,256,512]{3,2,0,1:T(8,128)(2,1)S(1)}, u32[]{:S(2)}, u32[]{:S(2)}) collective-permute-start(bf16[4,2,256,512]{3,2,0,1:T(8,128)(2,1)S(1)} %bitcast.183), channel_id=1, source_target_pairs={{0,4},{2,6},{4,0},{6,2},{8,12},{10,14},{12,8},{14,10},{16,20},{18,... | collective-permute-start | bytes 6291464 | tf_op jit(solution)/shard_map/ppermute | solution.py:23
  390.7 24.5 %collective-permute-start.16 = (bf16[4,256,512]{2,1,0:T(8,128)(2,1)S(1)}, bf16[4,256,512]{2,1,0:T(8,128)(2,1)S(1)}, u32[]{:S(2)}, u32[]{:S(2)}) collective-permute-start(bf16[4,256,512]{2,1,0:T(8,128)(2,1)S(1)} %slice_bitcast_fusion.2), channel_id=1, source_target_pairs={{0,4},{2,6},{4,0},{6,2},{8,12},{10,14},{12,8},{14,10},{16,20},{18,... | collective-permute-start | bytes 3145736 | tf_op jit(solution)/shard_map/ppermute | solution.py:23
  393.2 27.8 %collective-permute-start.21 = (bf16[4,256,512]{2,1,0:T(8,128)(2,1)S(1)}, bf16[4,256,512]{2,1,0:T(8,128)(2,1)S(1)}, u32[]{:S(2)}, u32[]{:S(2)}) collective-permute-start(bf16[4,256,512]{2,1,0:T(8,128)(2,1)S(1)} %slice_bitcast_fusion), channel_id=1, source_target_pairs={{0,2},{2,0},{4,6},{6,4},{8,10},{10,8},{12,14},{14,12},{16,18},{18,... | collective-permute-start | bytes 3145736 | tf_op jit(solution)/shard_map/ppermute | solution.py:23
  415.6 19.5 %collective-permute-start.17 = (bf16[256,512]{1,0:T(8,128)(2,1)S(1)}, bf16[256,512]{1,0:T(8,128)(2,1)S(1)}, u32[]{:S(2)}, u32[]{:S(2)}) collective-permute-start(bf16[256,512]{1,0:T(8,128)(2,1)S(1)} %get-tuple-element.85), channel_id=1, source_target_pairs={{0,24},{2,26},{4,28},{6,30},{8,0},{10,2},{12,4},{14,6},{16,8},{18,... | collective-permute-start | bytes 786440 | tf_op jit(solution)/shard_map/ppermute | solution.py:27
  416.2 20.6 %collective-permute-start.18 = (bf16[256,512]{1,0:T(8,128)(2,1)S(1)}, bf16[256,512]{1,0:T(8,128)(2,1)S(1)}, u32[]{:S(2)}, u32[]{:S(2)}) collective-permute-start(bf16[256,512]{1,0:T(8,128)(2,1)S(1)} %get-tuple-element.87), channel_id=1, source_target_pairs={{0,16},{2,18},{4,20},{6,22},{8,24},{10,26},{12,28},{14,30},{16,0},... | collective-permute-start | bytes 786440 | tf_op jit(solution)/shard_map/ppermute | solution.py:27
  418.6 32.9 %collective-permute-start.19 = (bf16[256,512]{1,0:T(8,128)(2,1)S(1)}, bf16[256,512]{1,0:T(8,128)(2,1)S(1)}, u32[]{:S(2)}, u32[]{:S(2)}) collective-permute-start(bf16[256,512]{1,0:T(8,128)(2,1)S(1)} %get-tuple-element.86), channel_id=1, source_target_pairs={{0,8},{2,10},{4,12},{6,14},{8,16},{10,18},{12,20},{14,22},{16,24},... | collective-permute-start | bytes 786440 | tf_op jit(solution)/shard_map/ppermute | solution.py:27
  421.3 40.8 %copy-start.3 = (f32[256,2048]{1,0:T(8,128)S(1)}, f32[256,2048]{1,0:T(8,128)}, u32[]{:S(2)}) copy-start(f32[256,2048]{1,0:T(8,128)} %copy-done.2) | copy-start | bytes 6291460
  421.4 37.2 %collective-permute-start.22 = (bf16[256,512]{1,0:T(8,128)(2,1)S(1)}, bf16[256,512]{1,0:T(8,128)(2,1)S(1)}, u32[]{:S(2)}, u32[]{:S(2)}) collective-permute-start(bf16[256,512]{1,0:T(8,128)(2,1)S(1)} %get-tuple-element.88), channel_id=1, source_target_pairs={{0,24},{2,26},{4,28},{6,30},{8,0},{10,2},{12,4},{14,6},{16,8},{18,... | collective-permute-start | bytes 786440 | tf_op jit(solution)/shard_map/ppermute | solution.py:27
  421.4 37.2 %collective-permute-start.23 = (bf16[256,512]{1,0:T(8,128)(2,1)S(1)}, bf16[256,512]{1,0:T(8,128)(2,1)S(1)}, u32[]{:S(2)}, u32[]{:S(2)}) collective-permute-start(bf16[256,512]{1,0:T(8,128)(2,1)S(1)} %get-tuple-element.90), channel_id=1, source_target_pairs={{0,16},{2,18},{4,20},{6,22},{8,24},{10,26},{12,28},{14,30},{16,0},... | collective-permute-start | bytes 786440 | tf_op jit(solution)/shard_map/ppermute | solution.py:27
  435.1 26.9 %collective-permute-start.24 = (bf16[256,512]{1,0:T(8,128)(2,1)S(1)}, bf16[256,512]{1,0:T(8,128)(2,1)S(1)}, u32[]{:S(2)}, u32[]{:S(2)}) collective-permute-start(bf16[256,512]{1,0:T(8,128)(2,1)S(1)} %get-tuple-element.89), channel_id=1, source_target_pairs={{0,8},{2,10},{4,12},{6,14},{8,16},{10,18},{12,20},{14,22},{16,24},... | collective-permute-start | bytes 786440 | tf_op jit(solution)/shard_map/ppermute | solution.py:27
Sparse Core Ops, SparseCore 0:
  66.4 20.5 all-reduce.1
  306.2 32.9 reduce-scatter.1
